TPU v7x, 512 devices: a whole 4x4x16 slice. The times are simulated.
512 devices in a mesh: dp: 64 (over x, z_lo, core), tensor: 8 (over z_hi, y).
Axes of the slice: x: 4, y: 4, z: 16 (z_hi: 2, z_lo: 8; z = z_hi * 8 + z_lo), core: 2. Of those that a mesh axis runs over, the one named last changes fastest.
Arguments:
- image_pooled: bfloat16 [8192, 1408], P('dp'), may hold values from -6 to 6
- text_pooled: bfloat16 [8192, 1408], P('dp'), may hold values from -6 to 6
- image_proj: bfloat16 [1152, 1408], P('tensor'), may hold values from -0.15625 to 0.15625
- text_proj: bfloat16 [1152, 1408], P('tensor'), may hold values from -0.15625 to 0.15625
- logit_scale: float32 [], replicated, may hold values from 4 to 12
- logit_bias: float32 [], replicated, may hold values from -5 to -1
Outputs:
- loss: float32 [], replicated
- grad_scale: float32 [], replicated
- grad_bias: float32 [], replicated
- grad_image_proj: float32 [1152, 1408], P('tensor')
- grad_text_proj: float32 [1152, 1408], P('tensor')
All inputs are finite; a program needn't handle non-finite values.
Results may differ from a plain program's by a relative error of at most 0.004.
Values may be sent and summed in bfloat16 or wider, within the bound.
No kernel may reach another device: no remote copies, remote signals or barrier semaphores. Data moves between devices by JAX's collectives and lax.ppermute only.
A program may use at most 64 MiB of HBM per device.

v0:
```python
import jax
import jax.numpy as jnp
from jax import lax
from jax.sharding import PartitionSpec as P

eps = 1e-06


def from_behind(block, axis, distance):
    devices = range(lax.axis_size(axis))
    route = [((i - distance) % len(devices), i) for i in devices]
    return lax.ppermute(block, axis, route)


def shards(image_pooled, text_pooled, image_proj, text_proj, logit_scale, logit_bias):
    groups = lax.axis_size("dp")
    group = lax.axis_index("dp")
    member = lax.axis_index("tensor")
    rows = image_pooled.shape[0]
    total = rows * groups
    slice_rows = rows // lax.axis_size("tensor")
    image_raw = lax.dot_general(
        image_pooled, image_proj, (((1,), (1,)), ((), ())), preferred_element_type=jnp.float32
    )
    text_raw = lax.dot_general(
        text_pooled, text_proj, (((1,), (1,)), ((), ())), preferred_element_type=jnp.float32
    )
    image_sq, text_sq = lax.psum(
        (jnp.sum(image_raw * image_raw, axis=1), jnp.sum(text_raw * text_raw, axis=1)), "tensor"
    )
    image_norm = jnp.sqrt(image_sq + eps)[:, None]
    text_norm = jnp.sqrt(text_sq + eps)[:, None]
    image_unit = image_raw / image_norm
    text_unit = text_raw / text_norm
    image_full = lax.all_gather(image_unit.astype(jnp.bfloat16), "tensor", axis=1, tiled=True)
    text_slice = lax.all_to_all(
        text_unit.astype(jnp.bfloat16), "tensor", split_axis=0, concat_axis=1, tiled=True
    )
    rowpos = jnp.arange(rows, dtype=jnp.int32)
    slot = member * slice_rows + jnp.arange(slice_rows, dtype=jnp.int32)
    width = image_full.shape[1]

    def tile(visiting, anchors, slots, sums, image_demb):
        loss, grad_scale, grad_bias = sums
        dots = lax.dot_general(
            image_full, visiting, (((1,), (1,)), ((), ())), preferred_element_type=jnp.float32
        )
        logits = logit_scale * dots + logit_bias
        match = (anchors[None, :] == group) & (rowpos[:, None] == slots[None, :])
        label = jnp.where(match, jnp.float32(1.0), jnp.float32(-1.0))
        loss = loss - jnp.sum(jax.nn.log_sigmoid(label * logits)) / total
        pair_grad = -label * jax.nn.sigmoid(-label * logits) / total
        grad_scale = grad_scale + jnp.sum(pair_grad * dots)
        grad_bias = grad_bias + jnp.sum(pair_grad)
        coef = (logit_scale * pair_grad).astype(jnp.bfloat16)
        image_demb = image_demb + jnp.dot(coef, visiting, preferred_element_type=jnp.float32)
        visit_grad = lax.dot_general(
            coef, image_full, (((0,), (0,)), ((), ())), preferred_element_type=jnp.float32
        )
        return ((loss, grad_scale, grad_bias), image_demb, visit_grad)

    zero = jnp.float32(0.0)
    start_sums = (zero, zero, zero)
    start_demb = jnp.zeros((rows, width), jnp.float32)
    start_grad = jnp.zeros((slice_rows, width), jnp.float32)

    def one_step(step, state):
        visiting, carried_grad, sums, image_demb = state
        anchors = jnp.full((slice_rows,), (group - step) % groups, jnp.int32)
        sums, image_demb, visit_grad = tile(visiting, anchors, slot, sums, image_demb)
        carried_grad = carried_grad + visit_grad
        visiting = from_behind(visiting, "dp", 1)
        carried_grad = from_behind(carried_grad, "dp", 1)
        return (visiting, carried_grad, sums, image_demb)

    state = lax.fori_loop(0, groups, one_step, (text_slice, start_grad, start_sums, start_demb))
    text_demb, sums, image_demb = (state[1], state[2], state[3])
    loss, grad_scale, grad_bias = lax.psum((sums[0], sums[1], sums[2]), ("dp", "tensor"))
    image_dcols = lax.psum_scatter(image_demb, "tensor", scatter_dimension=1, tiled=True)
    text_dcols = lax.all_to_all(text_demb, "tensor", split_axis=1, concat_axis=0, tiled=True)
    image_inner, text_inner = lax.psum(
        (jnp.sum(image_unit * image_dcols, axis=1), jnp.sum(text_unit * text_dcols, axis=1)),
        "tensor",
    )
    image_dlow = ((image_dcols - image_unit * image_inner[:, None]) / image_norm).astype(
        jnp.bfloat16
    )
    text_dlow = ((text_dcols - text_unit * text_inner[:, None]) / text_norm).astype(jnp.bfloat16)
    image_wpart = lax.dot_general(
        image_dlow, image_pooled, (((0,), (0,)), ((), ())), preferred_element_type=jnp.float32
    )
    text_wpart = lax.dot_general(
        text_dlow, text_pooled, (((0,), (0,)), ((), ())), preferred_element_type=jnp.float32
    )
    grad_image_proj, grad_text_proj = lax.psum((image_wpart, text_wpart), "dp")
    return (loss, grad_scale, grad_bias, grad_image_proj, grad_text_proj)


def solution(mesh):
    placed = (P("dp", None), P("dp", None), P("tensor", None), P("tensor", None), P(), P())
    return jax.shard_map(
        shards,
        mesh=mesh,
        in_specs=placed,
        out_specs=(P(), P(), P(), P("tensor", None), P("tensor", None)),
        check_vma=False,
    )
```

profile of v0, /device:TPU:1, one launch (start us, length us, event | category | flops | bytes accessed | tf_op | source)
XLA Modules:
  0.0 2299.2 jit_solution(7903026155618589024)
XLA Ops:
  9.8 46.7 %all-reduce.3 = (f32[128]{0:T(128)S(1)}, f32[128]{0:T(128)S(1)}) all-reduce(f32[128]{0:T(128)S(1)} %get-tuple-element.454, f32[128]{0:T(128)S(1)} %get-tuple-element.456), channel_id=1, replica_groups=mesh['dp'=64,'tensor'=8] {'tensor'}, use_global_device_ids=true, to_apply=%region_1.0 | all-reduce | flops 256 | bytes 2048 | tf_op jit(solution)/shard_map/psum | solution.py:28
  61.4 57.5 %all_gather.3 = bf16[128,1152]{0,1:T(8,128)(2,1)S(1)} all-gather(bf16[128,144]{0,1:T(8,128)(2,1)S(1)} %fusion.20), channel_id=1, replica_groups=mesh['dp'=64,'tensor'=8] {'tensor'}, dimensions={1}, use_global_device_ids=true | all-gather | bytes 331776 | tf_op jit(solution)/shard_map/all_gather | solution.py:35
  119.2 1196.1 %while.26 = (s32[]{:T(128)}, bf16[16,1152]{1,0:T(8,128)(2,1)S(1)}, f32[16,1152]{1,0:T(8,128)S(1)}, f32[]{:T(128)}, f32[]{:T(128)}, /*index=5*/f32[]{:T(128)}, f3...) while((s32[]{:T(128)}, bf16[16,1152]{1,0:T(8,128)(2,1)S(1)}, ...), condition=%wide.region_8.9_spmd.clone, body=%wide.region_4.8_spmd.clone.sunk | while | flops 14526498 | bytes 2531930 | solution.py:76
  119.3 13.8 collective-permute-start
  164.5 5.8 collective-permute-done
  183.2 5.8 collective-permute-done
  201.9 5.8 collective-permute-done
  220.6 5.8 collective-permute-done
  239.3 5.8 collective-permute-done
  258.0 5.8 collective-permute-done
  276.7 5.8 collective-permute-done
  295.4 5.8 collective-permute-done
  314.1 5.8 collective-permute-done
  332.8 5.8 collective-permute-done
  351.5 5.8 collective-permute-done
  370.2 5.8 collective-permute-done
  388.9 5.8 collective-permute-done
  407.6 5.8 collective-permute-done
  426.3 5.8 collective-permute-done
  1316.6 27.2 %all_to_all.38 = f32[16,8,144]{2,0,1:T(8,128)S(1)} all-to-all(f32[16,8,144]{2,0,1:T(8,128)S(1)} %copy.25), channel_id=1, replica_groups=mesh['dp'=64,'tensor'=8] {'tensor'}, dimensions={1} | all-to-all | bytes 147456 | tf_op jit(solution)/shard_map/all_to_all | solution.py:80
  1344.0 93.7 %reduce-scatter.2.cloned.1.call-done = f32[128,144]{0,1:T(8,128)} async-done(((f32[128,1152]{0,1:T(8,128)}), f32[128,144]{0,1:T(8,128)}) %reduce-scatter.2.cloned.1.call-update) | async-done | bytes 73744 | tf_op jit(solution)/shard_map/reduce_scatter | solution.py:79
  1438.6 31.1 %all-reduce.2 = (f32[128]{0:T(128)S(1)}, f32[128]{0:T(128)S(1)}) all-reduce(f32[128]{0:T(128)S(1)} %multiply_reduce_fusion.3, f32[128]{0:T(128)S(1)} %multiply_reduce_fusion.2), channel_id=1, replica_groups=mesh['dp'=64,'tensor'=8] {'tensor'}, use_global_device_ids=true, to_apply=%region_14.15 | all-reduce | flops 256 | bytes 2048 | tf_op jit(solution)/shard_map/psum | solution.py:81
  1472.1 110.9 %all-reduce = (f32[]{:T(128)}, f32[]{:T(128)}, f32[]{:T(128)}) all-reduce(f32[]{:T(128)} %get-tuple-element.324, f32[]{:T(128)} %get-tuple-element.325, f32[]{:T(128)} %get-tuple-element.326), channel_id=1, replica_groups=mesh['dp'=64,'tensor'=8] {'dp','tensor'}, use_global_device_ids=true, to_apply=%region_9.10 | all-reduce | flops 3 | bytes 24 | tf_op jit(solution)/shard_map/psum | solution.py:78
  1583.0 706.3 %all-reduce.6.cloned.1.call-done = (f32[144,1408]{1,0:T(8,128)}, f32[144,1408]{1,0:T(8,128)}) async-done(((f32[144,1408]{1,0:T(8,128)}, f32[144,1408]{1,0:T(8,128)}), (f32[144,1408]{1,0:T(8,128)}, f32[144,1408]{1,0:T(8,128)})) %all-reduce.6.cloned.1.call-update) | async-done | bytes 1622032 | tf_op jit(solution)/shard_map/psum | solution.py:95
  (600 shorter events, 982.9 us)
Async XLA Ops:
  57.2 61.8 %all-to-all-start = ((bf16[8,16,144]{2,1,0:T(8,128)(2,1)}), bf16[8,16,144]{2,1,0:T(8,128)(2,1)S(1)}, u32[]{:S(2)}, u32[]{:S(2)}) async-start(bf16[8,16,144]{2,1,0:T(8,128)(2,1)} %bitcast), calls=%async_computation | async-start | bytes 131072 | tf_op jit(solution)/shard_map/all_to_all | solution.py:36
  60.6 1377.1 %reduce-scatter.2.cloned.1.call-start = ((), (), s32[]{:S(2)}) async-start(), calls=%async_computation.3 | async-start | bytes 663552 | tf_op jit(solution)/shard_map/reduce_scatter | solution.py:79
  119.3 20.4 collective-permute-start
  160.3 14.4 collective-permute-start.1
  179.0 14.4 collective-permute-start.1
  197.7 14.4 collective-permute-start.1
  216.4 14.4 collective-permute-start.1
  235.1 14.4 collective-permute-start.1
  253.8 14.4 collective-permute-start.1
  272.5 14.4 collective-permute-start.1
  291.2 14.4 collective-permute-start.1
  309.9 14.4 collective-permute-start.1
  328.6 14.4 collective-permute-start.1
  347.3 14.4 collective-permute-start.1
  366.0 14.4 collective-permute-start.1
  384.7 14.4 collective-permute-start.1
  403.4 14.4 collective-permute-start.1
  422.1 14.4 collective-permute-start.1
  440.8 14.4 collective-permute-start.1
  459.5 14.4 collective-permute-start.1
  478.2 14.4 collective-permute-start.1
  496.9 14.4 collective-permute-start.1
  515.6 14.4 collective-permute-start.1
  1316.4 972.9 %all-reduce.6.cloned.1.call-start = ((), (), s32[]{:S(2)}) async-start(), calls=%async_computation.4 | async-start | bytes 3244032 | tf_op jit(solution)/shard_map/psum | solution.py:95
  (113 other events, 1528.8 us)
Sparse Core Ops, SparseCore 0:
  1316.6 121.1 reduce-scatter.1
  1472.2 817.0 all-reduce.5
where the time goes:
time: 2310 us; the launch traced here: 2300 us
  waiting for transfers between devices  1440 us (62%)
  blocking collectives  273 us (12%)
  starting transfers between devices  262 us (11%)
  matrix products  176 us (8%)
  loops' own time  127 us (5%)
    psum x1, waiting for transfers between devices, shards(): grad_image_proj, grad_text_proj = lax.psum((image_wpart, text_wpart), 'dp')  706 us
    ppermute x128, waiting for transfers between devices, from_behind(): return lax.ppermute(block, axis, route)  638 us
    ppermute x128, starting transfers between devices, from_behind(): return lax.ppermute(block, axis, route)  258 us
    dot_general x64, matrix products, tile(): lax.dot_general(image_full, visiting, (((1,), (1,)), ((), ())), preferred...  141 us
    another operation x1, loops' own time, shards(): lax.fori_loop(0, groups, one_step, (text_slice, start_grad, start_sums, s...  127 us
    psum x1, blocking collectives, shards(): lax.psum((sums[0], sums[1], sums[2]), ('dp', 'tensor'))  111 us
    reduce_scatter x1, waiting for transfers between devices, shards(): lax.psum_scatter(image_demb, 'tensor', scatter_dimension=1, tiled=True)  93.7 us
    all_gather x1, blocking collectives, shards(): lax.all_gather(image_unit.astype(jnp.bfloat16), 'tensor', axis=1, tiled=T...  57.5 us
  transfers between devices with their start and end apart: 131, of which 128 were waited for; matrix products, arithmetic and copies ran while one was open for 8% of the time, Pallas kernels for 0%

commit v1 on v0

v1 whole, which is shorter than its diff:
```python
import jax
import jax.numpy as jnp
from jax import lax
from jax.sharding import Mesh, PartitionSpec as P

eps = 1e-06
X, ZL, CORE, ZH, Y = 4, 8, 2, 2, 4
AXES = ("x", "zl", "core", "zh", "y")


def swap(block, axis):
    return lax.ppermute(block, axis, [(0, 1), (1, 0)])


def by_core(block):
    other = swap(block, "core")
    first = lax.axis_index("core") == 0
    return jnp.stack([jnp.where(first, block, other), jnp.where(first, other, block)])


def spread(block, axes, count):
    copies = jnp.broadcast_to(block[None], (count,) + block.shape)
    return lax.all_to_all(copies, axes, 0, 0, tiled=True)


def in_parts(value):
    high = value.astype(jnp.bfloat16)
    rest = value - high.astype(jnp.float32)
    mid = rest.astype(jnp.bfloat16)
    low = (rest - mid.astype(jnp.float32)).astype(jnp.bfloat16)
    return jnp.stack([high, mid, low])


def shards(image_pooled, text_pooled, image_proj, text_proj, logit_scale, logit_bias):
    bf16, f32 = jnp.bfloat16, jnp.float32
    x, zl, core, zh, y = [lax.axis_index(a) for a in AXES]
    rows, width = image_pooled.shape
    feats = image_proj.shape[0]
    total = rows * X * ZL * CORE
    half, quarter, eighth = rows // ZH, rows // Y, rows // (Y * ZH)
    fhalf = feats // CORE
    emb = feats * ZH * Y

    image_rows = lax.dynamic_slice_in_dim(image_pooled, zh * half, half, 0)
    image_rows = lax.all_gather(image_rows, ("x", "core"), axis=0, tiled=True)
    text_rows = lax.dynamic_slice_in_dim(text_pooled, y * quarter + zh * eighth, eighth, 0)
    text_rows = lax.all_gather(text_rows, ("zh", "zl"), axis=0, tiled=True)
    text_rows = by_core(text_rows).reshape(CORE, ZH, ZL, eighth, width)
    text_rows = text_rows.transpose(2, 0, 1, 3, 4).reshape(ZL * CORE * quarter, width)

    def raw_of(proj, pooled):
        return lax.dot_general(
            proj, pooled, (((1,), (1,)), ((), ())), preferred_element_type=f32
        ).astype(bf16)

    image_raw = raw_of(image_proj, image_pooled)
    text_raw = raw_of(text_proj, text_pooled)
    image_raw = image_raw.reshape(CORE, fhalf, ZH, half).transpose(2, 1, 0, 3).reshape(ZH, fhalf, rows)
    mine = lax.dynamic_index_in_dim(image_raw, zh, 0, keepdims=False)
    away = lax.dynamic_index_in_dim(image_raw, 1 - zh, 0, keepdims=False)
    back = swap(away, "zh")
    text_raw = text_raw.reshape(Y, feats // Y, Y, quarter).transpose(2, 1, 0, 3)
    text_raw = lax.all_to_all(text_raw.reshape(Y * (feats // Y), rows), "y", 0, 0, tiled=True)
    text_raw = lax.all_gather(text_raw, ("zh", "zl"), axis=0, tiled=True)
    text_raw = by_core(text_raw).reshape(CORE, ZH, ZL, Y, feats // Y, Y, quarter)
    text_raw = text_raw.transpose(1, 3, 5, 4, 2, 0, 6).reshape(emb, ZL * CORE * quarter)

    low = zh == 0
    image_raw = jnp.concatenate([jnp.where(low, mine, back), jnp.where(low, back, mine)], 0)
    image_raw = spread(image_raw, ("x", "y"), X * Y)
    image_raw = by_core(image_raw).reshape(CORE, X, Y, ZH, fhalf, CORE, half)
    image_raw = image_raw.transpose(3, 2, 5, 4, 1, 0, 6).reshape(emb, X * CORE * half)

    n_images, n_texts = image_raw.shape[1], text_raw.shape[1]
    wide = image_raw.astype(f32)
    image_inv = 1.0 / jnp.sqrt(jnp.sum(wide * wide, axis=0) + eps)
    wide = text_raw.astype(f32)
    text_inv = 1.0 / jnp.sqrt(jnp.sum(wide * wide, axis=0) + eps)

    i = jnp.arange(n_images, dtype=jnp.int32)
    j = jnp.arange(n_texts, dtype=jnp.int32)
    ix, icore, irow = i // (CORE * half), i // half % CORE, i % half
    jz, jcore, jrow = j // (CORE * quarter), j // quarter % CORE, j % quarter
    image_id = ((ix * ZL + zl) * CORE + icore) * rows + zh * half + irow
    text_id = ((x * ZL + jz) * CORE + jcore) * rows + y * quarter + jrow

    dots = lax.dot_general(
        image_raw, text_raw, (((0,), (0,)), ((), ())), preferred_element_type=f32
    )
    dots = dots * (image_inv[:, None] * text_inv[None, :])
    logits = logit_scale * dots + logit_bias
    label = jnp.where(image_id[:, None] == text_id[None, :], f32(1.0), f32(-1.0))
    loss = -jnp.sum(jax.nn.log_sigmoid(label * logits)) / total
    pair_grad = -label * jax.nn.sigmoid(-label * logits) / total
    grad_scale = jnp.sum(pair_grad * dots)
    grad_bias = jnp.sum(pair_grad)
    coef = logit_scale * pair_grad
    inner = coef * dots
    image_inner = jnp.sum(inner, axis=1)
    text_inner = jnp.sum(inner, axis=0)

    def own(raw):
        raw = raw.reshape(ZH * Y, feats, raw.shape[1])
        return lax.dynamic_slice_in_dim(raw, core * fhalf, fhalf, 1).reshape(emb // CORE, -1)

    image_own, text_own = own(image_raw), own(text_raw)
    image_draw = lax.dot_general(
        text_own, (coef * text_inv[None, :]).astype(bf16), (((1,), (1,)), ((), ())),
        preferred_element_type=f32,
    )
    image_draw = (image_draw - image_own.astype(f32) * (image_inner * image_inv)) * image_inv
    text_draw = jnp.dot(
        image_own, (coef * image_inv[:, None]).astype(bf16), preferred_element_type=f32
    )
    text_draw = (text_draw - text_own.astype(f32) * (text_inner * text_inv)) * text_inv
    image_w = jnp.dot(image_draw.astype(bf16), image_rows, preferred_element_type=f32)
    text_w = jnp.dot(text_draw.astype(bf16), text_rows, preferred_element_type=f32)

    sums = jnp.concatenate([in_parts(v) for v in (loss, grad_scale, grad_bias)])
    tail = jnp.zeros((8, width), bf16).at[0, :9].set(sums)
    tail = jnp.broadcast_to(tail, (X, Y, 8, width))
    parts = jnp.concatenate([image_w.astype(bf16), text_w.astype(bf16)])
    parts = jnp.concatenate([parts.reshape(X, Y, fhalf, width), tail], axis=2)
    parts = lax.all_to_all(
        parts.reshape(X * Y, fhalf + 8, width), ("x", "y"), 0, 0, tiled=True
    )
    parts = jnp.sum(parts.astype(f32), axis=0)
    tiles = parts[:fhalf].reshape(fhalf // 8, 8, width // 128, 128).transpose(0, 2, 1, 3)
    count = (fhalf // 8) * (width // 128)
    share = -(-count // ZL)
    tiles = jnp.pad(tiles.reshape(count, 8, 128), ((0, share * ZL - count), (0, 0), (0, 0)))
    tail = jnp.broadcast_to(parts[None, None, fhalf:, :128], (ZL, 1, 8, 128))
    tiles = jnp.concatenate([tiles.reshape(ZL, share, 8, 128), tail], axis=1)
    tiles = lax.all_to_all(tiles, "zl", 0, 0, tiled=True)
    tiles = jnp.sum(tiles, axis=0)
    tiles = tiles + swap(tiles, "zh")
    sums = tiles[share, 0, :9].reshape(3, 3).sum(axis=1)
    tiles = spread(tiles[:share], "zl", ZL)
    pieces = []
    for steps in (((0, 1), (2, 3)), ((0, 3), (2, 1)), ((0, 2), (2, 0))):
        route = [((s + h) * ZH + h, ((t + h) % X) * ZH + h) for s, t in steps for h in range(ZH)]
        pieces.append(lax.ppermute(tiles, ("x", "zh"), route))
    near, far, across = pieces
    place = (x - zh) % X
    image_g = jnp.where(place == 0, tiles, jnp.where(place == 1, near, jnp.where(place == 2, across, far)))
    text_g = jnp.where(place == 2, tiles, jnp.where(place == 3, near, jnp.where(place == 0, across, far)))
    both = jnp.stack([image_g, text_g]).reshape(2, ZL * share, 8, 128)[:, :count]
    both = by_core(both).reshape(CORE, 2, fhalf // 8, width // 128, 8, 128)
    both = both.transpose(1, 0, 2, 4, 3, 5).reshape(2, feats, width)
    return (sums[0], sums[1], sums[2], both[0], both[1])


def solution(mesh):
    fine = Mesh(mesh.devices.reshape(X, ZL, CORE, ZH, Y), AXES)
    dp, tensor = ("x", "zl", "core"), ("zh", "y")
    placed = (P(dp, None), P(dp, None), P(tensor, None), P(tensor, None), P(), P())
    return jax.shard_map(
        shards,
        mesh=fine,
        in_specs=placed,
        out_specs=(P(), P(), P(), P(tensor, None), P(tensor, None)),
        check_vma=False,
    )
```

time: 2310 us -> 407 us (0.18)
  waiting for transfers between devices: 1440 us -> 20.5 us
  starting transfers between devices: 262 us -> 71.2 us
  matrix products: 176 us -> 16.4 us
  loops' own time: 127 us -> 0 us
  blocking collectives: 273 us -> 153 us
  local copies, waits for them, and re-layouts: 6.67 us -> 101 us
    psum x1 -> x0, waiting for transfers between devices: 706 us -> none  [shards(): grad_image_proj, grad_text_proj = lax.psum((image_wpart, text_wpart), 'dp')]
    ppermute x128 -> x9, waiting for transfers between devices: 638 us -> 17.6 us  [the longest x3 9.71 us: shards(): pieces.append(lax.ppermute(tiles, ('x', 'zh'), route))]
    ppermute x128 -> x9, starting transfers between devices: 258 us -> 62.3 us  [the longest x6 51.9 us: swap(): return lax.ppermute(block, axis, [(0, 1), (1, 0)])]
    psum x3 -> x0, blocking collectives: 189 us -> none  [the longest x1 111 us: shards(): lax.psum((sums[0], sums[1], sums[2]), ('dp', 'tensor'))]
    dot_general x196 -> x5, matrix products: 176 us -> 16.4 us  [the longest x1 5.34 us: shards(): lax.dot_general(image_raw, text_raw, (((0,), (0,)), ((), ())), preferred_...]
    another operation x1 -> x0, loops' own time: 127 us -> none  [shards(): lax.fori_loop(0, groups, one_step, (text_slice, start_grad, start_sums, s...]
    reduce_scatter x1 -> x0, waiting for transfers between devices: 93.7 us -> none  [shards(): lax.psum_scatter(image_demb, 'tensor', scatter_dimension=1, tiled=True)]
    all_to_all x1 -> x3, blocking collectives: 27.2 us -> 104 us  [the longest x1 49.8 us: shards(): lax.all_to_all(parts.reshape(X * Y, fhalf + 8, width), ('x', 'y'), 0, 0,...]
  transfers between devices with their start and end apart: 131 -> 12, of which waited for: 128 -> 4; matrix products, arithmetic and copies ran while one was open for 8% -> 31% of each run, Pallas kernels for 0% -> 0%
where the time goes in v1:
time: 407 us; the launch traced here: 402 us
  blocking collectives  153 us (38%)
  local copies, waits for them, and re-layouts  101 us (25%)
  starting transfers between devices  71.2 us (17%)
  waiting for transfers between devices  20.5 us (5%)
  other arithmetic  19.4 us (5%)
  between operations  19.4 us (5%)
  matrix products  16.4 us (4%)
    ppermute x6, starting transfers between devices, swap(): return lax.ppermute(block, axis, [(0, 1), (1, 0)])  51.9 us
    all_to_all x1, blocking collectives, shards(): lax.all_to_all(parts.reshape(X * Y, fhalf + 8, width), ('x', 'y'), 0, 0,...  49.8 us
    all_to_all x1, blocking collectives, spread(): return lax.all_to_all(copies, axes, 0, 0, tiled=True)  28.4 us
    all_to_all x1, blocking collectives, shards(): tiles = lax.all_to_all(tiles, 'zl', 0, 0, tiled=True)  25.6 us
    all_gather x1, blocking collectives, shards(): text_rows = lax.all_gather(text_rows, ('zh', 'zl'), axis=0, tiled=True)  25.5 us
    transpose x2, local copies, waits for them, and re-layouts, shards(): text_raw.transpose(1, 3, 5, 4, 2, 0, 6).reshape(emb, ZL * CORE * quarter)  24.6 us
    all_gather x1, blocking collectives, shards(): text_raw = lax.all_gather(text_raw, ('zh', 'zl'), axis=0, tiled=True)  24.2 us
    another operation x4, local copies, waits for them, and re-layouts, by_core(): jnp.stack([jnp.where(first, block, other), jnp.where(first, other, block)])  18.5 us
  transfers between devices with their start and end apart: 12, of which 4 were waited for; matrix products, arithmetic and copies ran while one was open for 31% of the time, Pallas kernels for 0%

profile of v1, /device:TPU:1, one launch (start us, length us, event | category | flops | bytes accessed | tf_op | source)
XLA Modules:
  0.0 401.6 jit_solution(9676220487628900541)
XLA Ops:
  9.7 16.3 %collective-permute-start.1 = (bf16[72,128]{1,0:T(8,128)(2,1)S(1)}, bf16[72,128]{1,0:T(8,128)(2,1)S(1)}, u32[]{:S(2)}, u32[]{:S(2)}) collective-permute-start(bf16[72,128]{1,0:T(8,128)(2,1)S(1)} %dynamic-slice_bitcast_fusion), channel_id=1, source_target_pairs={{0,4},{4,0},{1,5},{5,1},{2,6},{6,2},{3,7},{7,3},{8,12},{12,8},{9,1... | collective-permute-start | bytes 55304 | tf_op jit(solution)/shard_map/ppermute | solution.py:12
  36.9 24.2 %all_gather.9 = bf16[2304,128]{1,0:T(8,128)(2,1)S(1)} all-gather(bf16[144,128]{1,0:T(8,128)(2,1)S(1)} %all_to_all.22), channel_id=1, replica_groups=mesh['x'=4,'zl'=8,'core'=2,'zh'=2,'y'=4] {'zh','zl'}, dimensions={0}, use_global_device_ids=true | all-gather | bytes 626688 | tf_op jit(solution)/shard_map/all_gather | solution.py:64
  61.1 10.4 %collective-permute-start = (bf16[2304,128]{1,0:T(8,128)(2,1)S(1)}, bf16[2304,128]{1,0:T(8,128)(2,1)S(1)}, u32[]{:S(2)}, u32[]{:S(2)}) collective-permute-start(bf16[2304,128]{1,0:T(8,128)(2,1)S(1)} %all_gather.9), channel_id=1, source_target_pairs={{0,8},{8,0},{1,9},{9,1},{2,10},{10,2},{3,11},{11,3},{4,12},{12,4},... | collective-permute-start | bytes 1769480 | tf_op jit(solution)/shard_map/ppermute | solution.py:12
  77.2 25.5 %all_gather.11 = bf16[256,1408]{1,0:T(8,128)(2,1)S(1)} all-gather(bf16[16,1408]{1,0:T(8,128)(2,1)S(1)} %constant_dynamic-slice_fusion), channel_id=1, replica_groups=mesh['x'=4,'zl'=8,'core'=2,'zh'=2,'y'=4] {'zh','zl'}, dimensions={0}, use_global_device_ids=true | all-gather | bytes 765952 | tf_op jit(solution)/shard_map/all_gather | solution.py:47
  102.7 7.7 %collective-permute-start.3 = (bf16[256,1408]{1,0:T(8,128)(2,1)S(1)}, bf16[256,1408]{1,0:T(8,128)(2,1)}, u32[]{:S(2)}, u32[]{:S(2)}) collective-permute-start(bf16[256,1408]{1,0:T(8,128)(2,1)S(1)} %all_gather.11), channel_id=1, source_target_pairs={{0,8},{8,0},{1,9},{9,1},{2,10},{10,2},{3,11},{11,3},{4,12},{12,4},... | collective-permute-start | bytes 2162696 | tf_op jit(solution)/shard_map/ppermute | solution.py:12
  115.6 7.7 %stack.72 = bf16[1,2,8,4,36,4,32]{4,3,2,1,6,5,0:T(4,128)(2,1)S(1)} reshape(bf16[2304,128]{0,1:T(8,128)(2,1)} %copy.66) | data formatting | bytes 1179648 | tf_op jit(solution)/shard_map/stack | solution.py:18
  125.4 7.9 %stack.73 = bf16[1,2,8,4,36,4,32]{4,3,2,1,6,5,0:T(4,128)(2,1)} reshape(bf16[2304,128]{0,1:T(8,128)(2,1)} %copy.67) | data formatting | bytes 1179648 | tf_op jit(solution)/shard_map/stack | solution.py:18
  133.3 6.7 %multiply_reduce_fusion = (f32[8,2,32]{0,2,1:T(8,128)S(1)}, bf16[2,4,4,36,8,2,32]{3,1,4,0,6,2,5:T(4,128)(2,1)S(1)}) fusion(bf16[1,2,8,4,36,4,32]{4,3,2,1,6,5,0:T(4,128)(2,1)} %stack.73, bf16[1,2,8,4,36,4,32]{4,3,2,1,6,5,0:T(4,128)(2,1)S(1)} %stack.72), kind=kLoop, calls=%fused_computation | loop fusion | flops 2358784 | bytes 2361344 | tf_op jit(solution)/shard_map/reduce_sum | solution.py:78
  142.0 7.4 %copy.71 = bf16[2,4,4,36,8,2,32]{3,2,1,0,6,5,4:T(4,128)(2,1)} copy(bf16[2,4,4,36,8,2,32]{3,1,4,0,6,2,5:T(4,128)(2,1)S(1)} %get-tuple-element.25) | data formatting | bytes 2359296 | tf_op jit(solution)/shard_map/transpose | solution.py:66
  149.4 17.1 %copy.68 = bf16[2,4,4,36,8,2,32]{6,5,4,3,2,1,0:T(2,128)(2,1)} copy(bf16[2,4,4,36,8,2,32]{3,1,4,0,6,2,5:T(4,128)(2,1)} %copy-done.2) | data formatting | bytes 2359296 | tf_op jit(solution)/shard_map/transpose | solution.py:66
  166.7 8.8 %reshape.258 = bf16[1152,512]{0,1:T(8,128)(2,1)} reshape(bf16[2,4,4,36,8,2,32]{3,2,1,0,6,5,4:T(4,128)(2,1)} %copy.71) | data formatting | bytes 2359296 | tf_op jit(solution)/shard_map/reshape | solution.py:66
  175.6 12.9 %reshape_reshape.6 = bf16[8,144,512]{2,1,0:T(8,128)(2,1)} reshape(bf16[2,4,4,36,8,2,32]{6,5,4,3,2,1,0:T(2,128)(2,1)} %copy.68) | data formatting | bytes 2359296 | tf_op jit(solution)/shard_map/reshape;reshape | solution.py:103
  195.5 6.0 %multiply_reduce_fusion.1 = (f32[4,2,64]{2,0,1:T(4,128)S(1)}, bf16[2,4,2,72,4,2,64]{6,2,3,0,1,4,5:T(2,128)(2,1)S(1)}) fusion(bf16[1,4,4,2,72,2,64]{6,5,4,3,2,1,0:T(2,128)(2,1)} %stack.76, bf16[1,4,4,2,72,2,64]{6,5,4,3,2,1,0:T(2,128)(2,1)} %stack.75), kind=kLoop, calls=%fused_computation.2 | loop fusion | flops 2358784 | bytes 2361344 | tf_op jit(solution)/shard_map/reduce_sum | solution.py:76
  201.5 6.7 %copy.70 = bf16[2,4,2,72,4,2,64]{3,2,1,0,6,5,4:T(2,128)(2,1)} copy(bf16[2,4,2,72,4,2,64]{6,2,3,0,1,4,5:T(2,128)(2,1)S(1)} %get-tuple-element.23) | data formatting | bytes 2359296 | tf_op jit(solution)/shard_map/transpose | solution.py:72
  212.1 7.6 %reshape.257 = bf16[1152,512]{0,1:T(8,128)(2,1)} reshape(bf16[2,4,2,72,4,2,64]{3,2,1,0,6,5,4:T(2,128)(2,1)} %copy.70) | data formatting | bytes 2359296 | tf_op jit(solution)/shard_map/reshape | solution.py:72
  219.7 5.3 %fusion.25 = (f32[512]{0:T(512)S(1)}, f32[]{:T(128)}, f32[512]{0:T(512)S(1)}, f32[]{:T(128)}, f32[]{:T(128)}, /*index=5*/f32[512,512]{1,0:T(8,128)}) fusion(f32[]{:T(128)S(6)} %mul.187, f32[]{:T(128)S(6)} %copy.80, f32[]{:T(128)S(6)} %copy.79, s32[512]{0:T(512)S(1)} %fusion.43, s32[512]{0:T(512)S(1)} %fusion.36, f32[512]{0:T(512)S(1)} %sqrt.13, ...), kind=kOutput, calls=%fused_computation.58 | convolution fusion | flops 611580928 | bytes 3420184 | tf_op jit(solution)/shard_map/dot_general | solution.py:87
  236.8 5.1 %convolution_convert_fusion.1 = bf16[576,1408]{1,0:T(8,128)(2,1)} fusion(bf16[512,1408]{1,0:T(8,128)(2,1)} %all-gather.2.cloned.1.call-done, bf16[576,512]{1,0:T(8,128)(2,1)} %bitcast.83, bf16[576,512]{1,0:T(8,128)(2,1)} %bitcast.81, f32[512]{0:T(512)S(1)} %sqrt.11, f32[512]{0:T(512)S(1)} %mul.192, f32[]{:T(128)S(6)} %mul.187, f32[512]{0:T(512)S(1)} %sqrt.13, ...), kind=kOutput, calls=%fused_computation.8 | convolution fusion | flops 1138155520 | bytes 5302284 | tf_op jit(solution)/shard_map/dot_general | solution.py:116
  243.9 49.8 %all_to_all.32 = bf16[16,80,1408]{2,1,0:T(8,128)(2,1)S(1)} all-to-all(bf16[16,80,1408]{2,1,0:T(8,128)(2,1)S(1)} %pad_maximum_fusion), channel_id=1, replica_groups=mesh['x'=4,'zl'=8,'core'=2,'zh'=2,'y'=4] {'x','y'}, dimensions={0} | all-to-all | bytes 7208960 | tf_op jit(solution)/shard_map/all_to_all | solution.py:124
  294.3 25.6 %all_to_all.33 = f32[8,14,8,128]{3,2,1,0:T(8,128)S(1)} all-to-all(f32[8,14,8,128]{3,2,1,0:T(8,128)S(1)} %pad_maximum_fusion.3), channel_id=1, replica_groups=mesh['x'=4,'zl'=8,'core'=2,'zh'=2,'y'=4] {'zl'}, dimensions={0} | all-to-all | bytes 917504 | tf_op jit(solution)/shard_map/all_to_all | solution.py:134
  319.9 6.8 %collective-permute-start.4 = (f32[14,8,128]{2,1,0:T(8,128)S(1)}, f32[14,8,128]{2,1,0:T(8,128)S(1)}, u32[]{:S(2)}, u32[]{:S(2)}) collective-permute-start(f32[14,8,128]{2,1,0:T(8,128)S(1)} %reduce_sum.98), channel_id=1, source_target_pairs={{0,4},{4,0},{1,5},{5,1},{2,6},{6,2},{3,7},{7,3},{8,12},{12,8},{9,1... | collective-permute-start | bytes 172040 | tf_op jit(solution)/shard_map/ppermute | solution.py:12
  326.8 6.8 %collective-permute-done.4 = f32[14,8,128]{2,1,0:T(8,128)S(1)} collective-permute-done((f32[14,8,128]{2,1,0:T(8,128)S(1)}, f32[14,8,128]{2,1,0:T(8,128)S(1)}, u32[]{:S(2)}, u32[]{:S(2)}) %collective-permute-start.4) | collective-permute-done | bytes 57376 | tf_op jit(solution)/shard_map/ppermute | solution.py:12
  333.6 28.4 %all_to_all.34 = f32[8,13,8,128]{3,2,1,0:T(8,128)S(1)} all-to-all(f32[8,13,8,128]{3,2,1,0:T(8,128)S(1)} %broadcast_in_dim.21), channel_id=1, replica_groups=mesh['x'=4,'zl'=8,'core'=2,'zh'=2,'y'=4] {'zl'}, dimensions={0} | all-to-all | bytes 851968 | tf_op jit(solution)/shard_map/all_to_all | solution.py:23
  372.5 9.7 %collective-permute-done.6 = f32[8,13,8,128]{3,2,1,0:T(8,128)S(1)} collective-permute-done((f32[8,13,8,128]{3,2,1,0:T(8,128)S(1)}, f32[8,13,8,128]{3,2,1,0:T(8,128)S(1)}, u32[]{:S(2)}, u32[]{:S(2)}) %collective-permute-start.6) | collective-permute-done | bytes 426016 | tf_op jit(solution)/shard_map/ppermute | solution.py:142
  382.4 8.8 %collective-permute-start.8 = (f32[2,99,8,128]{3,2,1,0:T(8,128)S(1)}, f32[2,99,8,128]{3,2,1,0:T(8,128)S(1)}, u32[]{:S(2)}, u32[]{:S(2)}) collective-permute-start(f32[2,99,8,128]{3,2,1,0:T(8,128)S(1)} %pad_maximum_fusion.2), channel_id=1, source_target_pairs={{0,8},{8,0},{1,9},{9,1},{2,10},{10,2},{3,11},{11,3},{4,12},{12,4},... | collective-permute-start | bytes 2433032 | tf_op jit(solution)/shard_map/ppermute | solution.py:12
  (93 shorter events, 63.1 us)
Async XLA Ops:
  7.2 1.0 copy-start
  7.2 25.3 %copy-start.5 = (bf16[128,1408]{1,0:T(8,128)(2,1)S(1)}, bf16[128,1408]{1,0:T(8,128)(2,1)}, u32[]{:S(2)}) copy-start(bf16[128,1408]{1,0:T(8,128)(2,1)} %param.8) | copy-start | bytes 1081348
  9.7 24.3 %collective-permute-start.1 = (bf16[72,128]{1,0:T(8,128)(2,1)S(1)}, bf16[72,128]{1,0:T(8,128)(2,1)S(1)}, u32[]{:S(2)}, u32[]{:S(2)}) collective-permute-start(bf16[72,128]{1,0:T(8,128)(2,1)S(1)} %dynamic-slice_bitcast_fusion), channel_id=1, source_target_pairs={{0,4},{4,0},{1,5},{5,1},{2,6},{6,2},{3,7},{7,3},{8,12},{12,8},{9,1... | collective-permute-start | bytes 55304 | tf_op jit(solution)/shard_map/ppermute | solution.py:12
  28.3 8.5 %all-to-all-start = ((bf16[4,36,128]{2,1,0:T(8,128)(2,1)}), bf16[4,36,128]{2,1,0:T(8,128)(2,1)S(1)}, u32[]{:S(2)}, u32[]{:S(2)}) async-start(bf16[4,36,128]{2,1,0:T(8,128)(2,1)} %reshape.265), calls=%async_computation | async-start | bytes 81920 | tf_op jit(solution)/shard_map/all_to_all | solution.py:63
  32.5 204.3 %all-gather.2.cloned.1.call-start = ((), (), s32[]{:S(2)}) async-start(), calls=%async_computation.5 | async-start | bytes 1622016 | tf_op jit(solution)/shard_map/all_gather | solution.py:45
  61.1 52.5 %collective-permute-start = (bf16[2304,128]{1,0:T(8,128)(2,1)S(1)}, bf16[2304,128]{1,0:T(8,128)(2,1)S(1)}, u32[]{:S(2)}, u32[]{:S(2)}) collective-permute-start(bf16[2304,128]{1,0:T(8,128)(2,1)S(1)} %all_gather.9), channel_id=1, source_target_pairs={{0,8},{8,0},{1,9},{9,1},{2,10},{10,2},{3,11},{11,3},{4,12},{12,4},... | collective-permute-start | bytes 1769480 | tf_op jit(solution)/shard_map/ppermute | solution.py:12
  72.5 39.3 %all-to-all-start.1 = ((bf16[16,144,128]{2,1,0:T(8,128)(2,1)}), bf16[16,144,128]{2,1,0:T(8,128)(2,1)}, u32[]{:S(2)}, u32[]{:S(2)}) async-start(bf16[16,144,128]{2,1,0:T(8,128)(2,1)} %broadcast_in_dim.18), calls=%async_computation.1 | async-start | bytes 1179648 | tf_op jit(solution)/shard_map/all_to_all | solution.py:23
  102.7 85.8 %collective-permute-start.3 = (bf16[256,1408]{1,0:T(8,128)(2,1)S(1)}, bf16[256,1408]{1,0:T(8,128)(2,1)}, u32[]{:S(2)}, u32[]{:S(2)}) collective-permute-start(bf16[256,1408]{1,0:T(8,128)(2,1)S(1)} %all_gather.11), channel_id=1, source_target_pairs={{0,8},{8,0},{1,9},{9,1},{2,10},{10,2},{3,11},{11,3},{4,12},{12,4},... | collective-permute-start | bytes 2162696 | tf_op jit(solution)/shard_map/ppermute | solution.py:12
  111.7 79.5 %collective-permute-start.2 = (bf16[16,144,128]{2,1,0:T(8,128)(2,1)}, bf16[16,144,128]{2,1,0:T(8,128)(2,1)}, u32[]{:S(2)}, u32[]{:S(2)}) collective-permute-start(bf16[16,144,128]{2,1,0:T(8,128)(2,1)} %all-to-all-done.1), channel_id=1, source_target_pairs={{0,8},{8,0},{1,9},{9,1},{2,10},{10,2},{3,11},{11,3},{4,12},{12,4},... | collective-permute-start | bytes 1769480 | tf_op jit(solution)/shard_map/ppermute | solution.py:12
  140.0 2.0 copy-start.2
  219.7 5.3 %copy-start.3 = (bf16[2,4,2,72,4,2,64]{6,5,4,3,2,1,0:T(2,128)(2,1)S(1)}, bf16[2,4,2,72,4,2,64]{6,5,4,3,2,1,0:T(2,128)(2,1)}, u32[]{:S(2)}) copy-start(bf16[2,4,2,72,4,2,64]{6,5,4,3,2,1,0:T(2,128)(2,1)} %copy.75) | copy-start | bytes 3538948
  227.5 5.9 %copy-start.4 = (bf16[8,2,2,16,1408]{4,3,2,1,0:T(8,128)(2,1)S(1)}, bf16[8,2,2,16,1408]{4,3,2,1,0:T(8,128)(2,1)}, u32[]{:S(2)}) copy-start(bf16[8,2,2,16,1408]{4,3,2,1,0:T(8,128)(2,1)} %copy.76) | copy-start | bytes 4325380
  319.9 13.6 %collective-permute-start.4 = (f32[14,8,128]{2,1,0:T(8,128)S(1)}, f32[14,8,128]{2,1,0:T(8,128)S(1)}, u32[]{:S(2)}, u32[]{:S(2)}) collective-permute-start(f32[14,8,128]{2,1,0:T(8,128)S(1)} %reduce_sum.98), channel_id=1, source_target_pairs={{0,4},{4,0},{1,5},{5,1},{2,6},{6,2},{3,7},{7,3},{8,12},{12,8},{9,1... | collective-permute-start | bytes 172040 | tf_op jit(solution)/shard_map/ppermute | solution.py:12
  362.0 10.5 %collective-permute-start.5 = (f32[8,13,8,128]{3,2,1,0:T(8,128)S(1)}, f32[8,13,8,128]{3,2,1,0:T(8,128)S(1)}, u32[]{:S(2)}, u32[]{:S(2)}) collective-permute-start(f32[8,13,8,128]{3,2,1,0:T(8,128)S(1)} %all_to_all.34), channel_id=1, source_target_pairs={{0,128},{132,260},{256,384},{388,4},{1,129},{133,261},{257,385},{3... | collective-permute-start | bytes 1277960 | tf_op jit(solution)/shard_map/ppermute | solution.py:142
  366.7 15.5 %collective-permute-start.6 = (f32[8,13,8,128]{3,2,1,0:T(8,128)S(1)}, f32[8,13,8,128]{3,2,1,0:T(8,128)S(1)}, u32[]{:S(2)}, u32[]{:S(2)}) collective-permute-start(f32[8,13,8,128]{3,2,1,0:T(8,128)S(1)} %all_to_all.34), channel_id=1, source_target_pairs={{0,256},{132,388},{256,0},{388,132},{1,257},{133,389},{257,1},{389... | collective-permute-start | bytes 1277960 | tf_op jit(solution)/shard_map/ppermute | solution.py:142
  371.1 11.1 %collective-permute-start.7 = (f32[8,13,8,128]{3,2,1,0:T(8,128)S(1)}, f32[8,13,8,128]{3,2,1,0:T(8,128)S(1)}, u32[]{:S(2)}, u32[]{:S(2)}) collective-permute-start(f32[8,13,8,128]{3,2,1,0:T(8,128)S(1)} %all_to_all.34), channel_id=1, source_target_pairs={{0,384},{132,4},{256,128},{388,260},{1,385},{133,5},{257,129},{389... | collective-permute-start | bytes 1277960 | tf_op jit(solution)/shard_map/ppermute | solution.py:142
  382.4 10.7 %collective-permute-start.8 = (f32[2,99,8,128]{3,2,1,0:T(8,128)S(1)}, f32[2,99,8,128]{3,2,1,0:T(8,128)S(1)}, u32[]{:S(2)}, u32[]{:S(2)}) collective-permute-start(f32[2,99,8,128]{3,2,1,0:T(8,128)S(1)} %pad_maximum_fusion.2), channel_id=1, source_target_pairs={{0,8},{8,0},{1,9},{9,1},{2,10},{10,2},{3,11},{11,3},{4,12},{12,4},... | collective-permute-start | bytes 2433032 | tf_op jit(solution)/shard_map/ppermute | solution.py:12
  393.2 1.4 copy-start.1
Sparse Core Ops, SparseCore 0:
  35.5 27.6 all-gather.1

commit v2 on v0

v2 whole, which is shorter than its diff:
```python
import jax
import jax.numpy as jnp
from jax import lax
from jax.experimental import pallas as pl
from jax.experimental.pallas import tpu as pltpu
from jax.sharding import Mesh, PartitionSpec as P

eps = 1e-06
X, ZL, CORE, ZH, Y = 4, 8, 2, 2, 4
AXES = ("x", "zl", "core", "zh", "y")
TAIL = 16


def swap(block, axis):
    return lax.ppermute(block, axis, [(0, 1), (1, 0)])


def spread(block, axes, count):
    copies = jnp.broadcast_to(block[None], (count,) + block.shape)
    return lax.all_to_all(copies, axes, 0, 0, tiled=True)


def in_parts(value):
    high = value.astype(jnp.bfloat16).astype(jnp.float32)
    rest = value - high
    mid = rest.astype(jnp.bfloat16).astype(jnp.float32)
    return high, mid, rest - mid


def pairs_kernel(
    place, factors, plane, ring_mine, ring_other, out, plane_raw, ring_raw
):
    bf16, f32 = jnp.bfloat16, jnp.float32
    core, x, y, zl, zh = [place[k] for k in range(5)]
    scale, bias = factors[0], factors[1]
    feats, rows = ring_mine.shape[1:]
    emb, block = ring_raw.shape
    own = emb // ZH
    total = rows * X * ZL * CORE

    for s in range(X * Y):
        for g in range(CORE):
            lanes = pl.ds((s // Y * CORE + g) * rows, rows)
            for h in range(ZH):
                piece = plane[s, pl.ds((g * ZH + h) * feats, feats), :]
                plane_raw[pl.ds((h * Y + s % Y) * feats, feats), lanes] = piece
    for ref, owner in ((ring_mine, core), (ring_other, 1 - core)):
        for s in range(ZH * ZL):
            at = (s // ZL * Y + s % Y) * feats
            lanes = pl.multiple_of((s % ZL // Y * CORE + owner) * rows, rows)
            ring_raw[pl.ds(at, feats), pl.ds(lanes, rows)] = ref[s]

    wide = ring_raw[...].astype(f32)
    ring_inv = 1.0 / jnp.sqrt(jnp.sum(wide * wide, axis=0, keepdims=True) + eps)
    own_at = pl.multiple_of(zh * own, 16)
    ring_own = ring_raw[pl.ds(own_at, own), :]

    lane = lax.broadcasted_iota(jnp.int32, (rows, block), 1)
    row = lax.broadcasted_iota(jnp.int32, (rows, block), 0)
    ring_id = ((x * ZL + 2 * y) * CORE + lane // rows) * rows + lane % rows
    loss = grad_scale = grad_bias = jnp.zeros((1, block), f32)
    for a in range(X * CORE):
        images = plane_raw[:, pl.ds(a * rows, rows)].T
        wide = images.astype(f32)
        inv = 1.0 / jnp.sqrt(jnp.sum(wide * wide, axis=1, keepdims=True) + eps)
        dots = jnp.dot(images, ring_raw[...], preferred_element_type=f32) * inv * ring_inv
        logits = scale * dots + bias
        plane_id = ((a // CORE * ZL + zl) * CORE + a % CORE) * rows + row
        label = jnp.where(plane_id == ring_id, f32(1.0), f32(-1.0))
        margin = label * logits
        small = jnp.exp(-jnp.abs(margin))
        sigmoid = jnp.where(margin >= 0, small, 1.0) / (1.0 + small)
        pair_grad = -label * sigmoid * f32(1.0 / total)
        inner = pair_grad * dots
        loss += jnp.sum(jnp.log1p(small) - jnp.minimum(margin, 0.0), axis=0, keepdims=True)
        grad_scale += jnp.sum(inner, axis=0, keepdims=True)
        grad_bias += jnp.sum(pair_grad, axis=0, keepdims=True)
        shift = scale * jnp.sum(inner, axis=1, keepdims=True) * inv
        shift = jnp.broadcast_to(shift, (rows, rows)).T[:1]
        inv = jnp.broadcast_to(inv, (rows, rows)).T[:1]
        coef = (scale * pair_grad * ring_inv).astype(bf16)
        draw = lax.dot_general(
            ring_own, coef, (((1,), (1,)), ((), ())), preferred_element_type=f32
        )
        raw = plane_raw[pl.ds(own_at, own), pl.ds(a * rows, rows)].astype(f32)
        draw = ((draw - raw * shift) * inv).astype(bf16)
        for b in range(Y):
            part = draw[b * feats : (b + 1) * feats]
            out[a // CORE * Y + b, pl.ds(0, feats), pl.ds(a % CORE * rows, rows)] = part

    lane = lax.broadcasted_iota(jnp.int32, (TAIL, CORE * rows), 1)
    tail = jnp.zeros((TAIL, CORE * rows), f32)
    for k, value in enumerate((loss * f32(1.0 / total), grad_scale, grad_bias)):
        for n, part in enumerate(in_parts(jnp.sum(value, axis=1, keepdims=True))):
            tail = jnp.where(lane == 3 * k + n, part, tail)
    for s in range(X * Y):
        out[s, pl.ds(feats, TAIL), :] = tail.astype(bf16)


def row_gradients(place, factors, plane, ring, ring_other):
    feats, rows = ring.shape[1:]
    smem, vmem = pl.BlockSpec(memory_space=pltpu.SMEM), pl.BlockSpec(memory_space=pltpu.VMEM)
    emb, block = feats * ZH * Y, rows * X
    return pl.pallas_call(
        pairs_kernel,
        out_shape=jax.ShapeDtypeStruct((X * Y, feats + TAIL, CORE * rows), jnp.bfloat16),
        in_specs=[smem] * 2 + [vmem] * 3,
        out_specs=vmem,
        scratch_shapes=[
            pltpu.VMEM((emb, CORE * block), jnp.bfloat16),
            pltpu.VMEM((emb, block), jnp.bfloat16),
        ],
        compiler_params=pltpu.CompilerParams(vmem_limit_bytes=48 * 1024 * 1024),
    )(place, factors, plane, ring, ring_other)


def shards(image_pooled, text_pooled, image_proj, text_proj, logit_scale, logit_bias):
    bf16, f32 = jnp.bfloat16, jnp.float32
    x, zl, core, zh, y = [lax.axis_index(a) for a in AXES]
    width = image_pooled.shape[1]
    feats = image_proj.shape[0]
    place = jnp.stack([core, x, y, zl, zh]).astype(jnp.int32)
    factors = jnp.stack([logit_scale, logit_bias])
    first = core == 0

    def raw_of(proj, pooled):
        return lax.dot_general(
            proj, pooled, (((1,), (1,)), ((), ())), preferred_element_type=f32
        ).astype(bf16)

    to_ring = [(p * Y + q, (p % 2 * Y + q) * Y + p // 2) for p in range(ZL) for q in range(Y)]
    pooled = jnp.where(first, image_pooled, text_pooled)
    beside = swap(jnp.where(first, text_pooled, image_pooled), "core")
    pooled = jnp.concatenate([jnp.where(first, pooled, beside), jnp.where(first, beside, pooled)])
    image_raw, text_raw = raw_of(image_proj, image_pooled), raw_of(text_proj, text_pooled)
    mine, theirs = jnp.where(first, image_raw, text_raw), jnp.where(first, text_raw, image_raw)
    raw = jnp.concatenate([mine, theirs])
    ring = lax.ppermute(raw, ("zl", "y"), to_ring)
    far = swap(raw, "zh")
    low = zh == 0

    def both_zh(here, there):
        return jnp.concatenate([jnp.where(low, here, there), jnp.where(low, there, here)])

    beside = swap(both_zh(theirs, far[feats:]), "core")
    ring_first, ring_second = ring[feats:], swap(ring[:feats], "core")
    plane = both_zh(mine, far[:feats])
    plane = jnp.concatenate([jnp.where(first, plane, beside), jnp.where(first, beside, plane)])
    plane, ring_first, ring_second = lax.optimization_barrier((plane, ring_first, ring_second))
    plane = spread(plane, ("x", "y"), X * Y)
    ring_first = lax.all_gather(ring_first, ("zh", "zl"), axis=0, tiled=False)
    ring_second = lax.all_gather(ring_second, ("zh", "zl"), axis=0, tiled=False)
    plane, ring_first, ring_second = lax.optimization_barrier((plane, ring_first, ring_second))
    parts = row_gradients(place, factors, plane, ring_first, ring_second)
    parts = lax.all_to_all(parts, ("x", "y"), 0, 0, tiled=True)
    parts = jnp.sum(parts.astype(f32), axis=0)
    draw, tail = parts[:feats].astype(bf16), parts[feats : feats + 8, :128]

    weight = jnp.dot(draw, pooled, preferred_element_type=f32)

    count = (feats // 8) * (width // 128)
    share = -(-count // (X * ZL))
    tiles = weight.reshape(feats // 8, 8, width // 128, 128).transpose(0, 2, 1, 3)
    tiles = jnp.pad(tiles.reshape(count, 8, 128), ((0, X * ZL * share - count), (0, 0), (0, 0)))
    tiles = lax.all_to_all(tiles.reshape(X, ZL * share, 8, 128), "x", 0, 0, tiled=True)
    tiles = jnp.sum(tiles, axis=0).reshape(ZL, share, 8, 128)
    tiles = jnp.concatenate([tiles, jnp.broadcast_to(tail, (ZL, 1, 8, 128))], axis=1)
    tiles = jnp.sum(lax.all_to_all(tiles, "zl", 0, 0, tiled=True), axis=0)
    tail = tiles[share]
    tail = jnp.where(first, tail, swap(tail, "core"))
    sums = tail[0, :9].reshape(3, 3).sum(axis=1)
    tiles = spread(tiles[:share].astype(bf16), "zl", ZL)
    tiles = lax.all_gather(tiles, "x", axis=0, tiled=False)
    other = swap(tiles, "core")

    def whole(tiles):
        tiles = tiles.reshape(X * ZL * share, 8, 128)[:count]
        tiles = tiles.reshape(feats // 8, width // 128, 8, 128).transpose(0, 2, 1, 3)
        return tiles.reshape(feats, width).astype(f32)

    image_grad = whole(jnp.where(first, tiles, other))
    text_grad = whole(jnp.where(first, other, tiles))
    return (sums[0], sums[1], sums[2], image_grad, text_grad)


def solution(mesh):
    fine = Mesh(mesh.devices.reshape(X, ZL, CORE, ZH, Y), AXES)
    dp, tensor = ("x", "zl", "core"), ("zh", "y")
    placed = (P(dp, None), P(dp, None), P(tensor, None), P(tensor, None), P(), P())
    return jax.shard_map(
        shards,
        mesh=fine,
        in_specs=placed,
        out_specs=(P(), P(), P(), P(tensor, None), P(tensor, None)),
        check_vma=False,
    )
```

time: 2310 us -> 214 us (0.09)
  waiting for transfers between devices: 1440 us -> 13.9 us
  blocking collectives: 273 us -> 93.7 us
  starting transfers between devices: 262 us -> 86.3 us
  matrix products: 176 us -> 2.97 us
  loops' own time: 127 us -> 0 us
    psum x1 -> x0, waiting for transfers between devices: 706 us -> none  [shards(): grad_image_proj, grad_text_proj = lax.psum((image_wpart, text_wpart), 'dp')]
    ppermute x128 -> x7, waiting for transfers between devices: 638 us -> 4.82 us  [the longest x6 4.81 us: swap(): return lax.ppermute(block, axis, [(0, 1), (1, 0)])]
    ppermute x128 -> x7, starting transfers between devices: 258 us -> 61.4 us  [the longest x6 60.8 us: swap(): return lax.ppermute(block, axis, [(0, 1), (1, 0)])]
    psum x3 -> x0, blocking collectives: 189 us -> none  [the longest x1 111 us: shards(): lax.psum((sums[0], sums[1], sums[2]), ('dp', 'tensor'))]
    dot_general x196 -> x3, matrix products: 176 us -> 2.97 us  [the longest x2 2.69 us: raw_of(): lax.dot_general(proj, pooled, (((1,), (1,)), ((), ())), preferred_element...]
    another operation x1 -> x0, loops' own time: 127 us -> none  [shards(): lax.fori_loop(0, groups, one_step, (text_slice, start_grad, start_sums, s...]
    reduce_scatter x1 -> x0, waiting for transfers between devices: 93.7 us -> none  [shards(): lax.psum_scatter(image_demb, 'tensor', scatter_dimension=1, tiled=True)]
    all_gather x1 -> x3, blocking collectives: 57.5 us -> 61.8 us  [the longest x1 26.5 us: shards(): ring_first = lax.all_gather(ring_first, ('zh', 'zl'), axis=0, tiled=False)]
  transfers between devices with their start and end apart: 131 -> 10, of which waited for: 128 -> 5; matrix products, arithmetic and copies ran while one was open for 8% -> 1% of each run, Pallas kernels for 0% -> 0%
where the time goes in v2:
time: 214 us; the launch traced here: 213 us
  blocking collectives  93.7 us (44%)
  starting transfers between devices  86.3 us (40%)
  waiting for transfers between devices  13.9 us (6%)
  Pallas kernels  6.35 us (3%)
  local copies, waits for them, and re-layouts  5.9 us (3%)
  matrix products  2.97 us (1%)
  between operations  2.24 us (1%)
    ppermute x6, starting transfers between devices, swap(): return lax.ppermute(block, axis, [(0, 1), (1, 0)])  60.8 us
    all_gather x1, blocking collectives, shards(): ring_first = lax.all_gather(ring_first, ('zh', 'zl'), axis=0, tiled=False)  26.5 us
    all_gather x1, blocking collectives, shards(): ring_second = lax.all_gather(ring_second, ('zh', 'zl'), axis=0, tiled=False)  25.5 us
    all_to_all x1, blocking collectives, shards(): tiles = jnp.sum(lax.all_to_all(tiles, 'zl', 0, 0, tiled=True), axis=0)  17.2 us
    all_to_all x1, blocking collectives, spread(): return lax.all_to_all(copies, axes, 0, 0, tiled=True)  14.7 us
    all_to_all x1, starting transfers between devices, spread(): return lax.all_to_all(copies, axes, 0, 0, tiled=True)  13.6 us
    all_gather x1, blocking collectives, shards(): tiles = lax.all_gather(tiles, 'x', axis=0, tiled=False)  9.75 us
    all_to_all x1, waiting for transfers between devices, shards(): lax.all_to_all(tiles.reshape(X, ZL * share, 8, 128), 'x', 0, 0, tiled=True)  9.04 us
  transfers between devices with their start and end apart: 10, of which 5 were waited for; matrix products, arithmetic and copies ran while one was open for 1% of the time, Pallas kernels for 0%

profile of v2, /device:TPU:1, one launch (start us, length us, event | category | flops | bytes accessed | tf_op | source)
XLA Modules:
  0.0 213.4 jit_solution(3956369265571930773)
XLA Ops:
  0.7 1.4 convolution_convert_fusion
  2.1 1.3 broadcast_select_fusion.9
  3.4 16.3 %collective-permute-start = (bf16[288,128]{1,0:T(8,128)(2,1)S(1)}, bf16[288,128]{1,0:T(8,128)(2,1)S(1)}, u32[]{:S(2)}, u32[]{:S(2)}) collective-permute-start(bf16[288,128]{1,0:T(8,128)(2,1)S(1)} %pad_maximum_fusion.2), channel_id=1, source_target_pairs={{0,4},{4,0},{1,5},{5,1},{2,6},{6,2},{3,7},{7,3},{8,12},{12,8},{9,1... | collective-permute-start | bytes 221192 | tf_op jit(solution)/shard_map/ppermute | solution.py:15
  20.3 1.3 collective-permute-done
  21.7 5.6 %collective-permute-start.1 = (bf16[288,128]{1,0:T(8,128)(2,1)S(1)}, bf16[288,128]{1,0:T(8,128)(2,1)S(1)}, u32[]{:S(2)}, u32[]{:S(2)}) collective-permute-start(bf16[288,128]{1,0:T(8,128)(2,1)S(1)} %pad_maximum_fusion.4), channel_id=1, source_target_pairs={{0,8},{8,0},{1,9},{9,1},{2,10},{10,2},{3,11},{11,3},{4,12},{12,4},... | collective-permute-start | bytes 221192 | tf_op jit(solution)/shard_map/ppermute | solution.py:15
  27.3 1.9 collective-permute-start.3
  29.3 1.1 collective-permute-done.3
  30.4 1.9 broadcast_in_dim.6
  32.3 13.6 %all-to-all-start = ((bf16[16,576,128]{2,1,0:T(8,128)(2,1)}), bf16[16,576,128]{2,1,0:T(8,128)(2,1)S(1)}, u32[]{:S(2)}, u32[]{:S(2)}) async-start(bf16[16,576,128]{2,1,0:T(8,128)(2,1)} %broadcast_in_dim.6), calls=%async_computation | async-start | bytes 4718592 | tf_op jit(solution)/shard_map/all_to_all | solution.py:20
  47.3 26.5 %all-gather = bf16[2304,128]{1,0:T(8,128)(2,1)S(1)} all-gather(bf16[144,128]{1,0:T(8,128)(2,1)S(1)} %get-tuple-element.12), channel_id=2, replica_groups=mesh['x'=4,'zl'=8,'core'=2,'zh'=2,'y'=4] {'zh','zl'}, dimensions={0}, use_global_device_ids=true | all-gather | bytes 626688 | tf_op jit(solution)/shard_map/all_gather | solution.py:151
  73.8 25.5 %all-gather.1 = bf16[2304,128]{1,0:T(8,128)(2,1)} all-gather(bf16[144,128]{1,0:T(8,128)(2,1)S(1)} %collective-permute-done.3), channel_id=3, replica_groups=mesh['x'=4,'zl'=8,'core'=2,'zh'=2,'y'=4] {'zh','zl'}, dimensions={0}, use_global_device_ids=true | all-gather | bytes 626688 | tf_op jit(solution)/shard_map/all_gather | solution.py:152
  100.4 6.3 %shard_map.101 = bf16[16,160,256]{2,1,0:T(8,128)(2,1)S(1)} custom-call(s32[5]{0:T(128)S(1)} %stack.32.place, f32[2]{0:T(128)S(1)} %pad_maximum_fusion.5.factors, bf16[16,576,128]{2,1,0:T(8,128)(2,1)S(1)} %all-to-all-done.plane, bf16[16,144,128]{2,1,0:T(8,128)(2,1)S(1)} %bitcast.44, bf16[16,144,128]{2,1,0:T(8,128)(2,1)S(1)} %bitcast.45), custom_call_target="tpu_custom_call" | custom-call | tf_op jit(solution)/shard_map/pallas_call | solution.py:104
  107.9 6.8 %all-to-all-start.1 = ((bf16[16,160,256]{2,1,0:T(8,128)(2,1)}), bf16[16,160,256]{2,1,0:T(8,128)(2,1)S(1)}, u32[]{:S(2)}, u32[]{:S(2)}) async-start(bf16[16,160,256]{2,1,0:T(8,128)(2,1)} %copy-done.1), calls=%async_computation.1 | async-start | bytes 2621440 | tf_op jit(solution)/shard_map/all_to_all | solution.py:155
  114.8 14.2 %collective-permute-start.4 = (bf16[128,1408]{1,0:T(8,128)(2,1)S(1)}, bf16[128,1408]{1,0:T(8,128)(2,1)S(1)}, u32[]{:S(2)}, u32[]{:S(2)}) collective-permute-start(bf16[128,1408]{1,0:T(8,128)(2,1)S(1)} %broadcast_select_fusion.4), channel_id=1, source_target_pairs={{0,8},{8,0},{1,9},{9,1},{2,10},{10,2},{3,11},{11,3},{4,12},{12,4},... | collective-permute-start | bytes 1081352 | tf_op jit(solution)/shard_map/ppermute | solution.py:15
  129.0 1.3 collective-permute-done.4
  131.9 4.4 %all-to-all-start.2 = ((f32[4,56,8,128]{3,2,1,0:T(8,128)}), f32[4,56,8,128]{3,2,1,0:T(8,128)S(1)}, u32[]{:S(2)}, u32[]{:S(2)}) async-start(f32[4,56,8,128]{3,2,1,0:T(8,128)} %bitcast.12), calls=%async_computation.2 | async-start | bytes 1835008 | tf_op jit(solution)/shard_map/all_to_all | solution.py:165
  136.3 9.0 %all-to-all-done.2 = f32[4,56,8,128]{3,2,1,0:T(8,128)S(1)} async-done(((f32[4,56,8,128]{3,2,1,0:T(8,128)}), f32[4,56,8,128]{3,2,1,0:T(8,128)S(1)}, u32[]{:S(2)}, u32[]{:S(2)}) %all-to-all-start.2) | async-done | bytes 917536 | tf_op jit(solution)/shard_map/all_to_all | solution.py:165
  145.4 17.2 %all_to_all.25 = f32[8,8,8,128]{3,2,1,0:T(8,128)S(1)} all-to-all(f32[8,8,8,128]{3,2,1,0:T(8,128)S(1)} %pad_maximum_fusion), channel_id=1, replica_groups=mesh['x'=4,'zl'=8,'core'=2,'zh'=2,'y'=4] {'zl'}, dimensions={0} | all-to-all | bytes 524288 | tf_op jit(solution)/shard_map/all_to_all | solution.py:168
  162.7 14.7 %all_to_all.26 = bf16[8,7,8,128]{3,2,1,0:T(8,128)(2,1)S(1)} all-to-all(bf16[8,7,8,128]{3,2,1,0:T(8,128)(2,1)S(1)} %broadcast_in_dim.8), channel_id=1, replica_groups=mesh['x'=4,'zl'=8,'core'=2,'zh'=2,'y'=4] {'zl'}, dimensions={0} | all-to-all | bytes 229376 | tf_op jit(solution)/shard_map/all_to_all | solution.py:20
  177.4 9.8 %all-gather.2 = bf16[32,7,8,128]{3,2,1,0:T(8,128)(2,1)S(1)} all-gather(bf16[8,7,8,128]{3,2,1,0:T(8,128)(2,1)S(1)} %all_to_all.26), channel_id=4, replica_groups=mesh['x'=4,'zl'=8,'core'=2,'zh'=2,'y'=4] {'x'}, dimensions={0}, use_global_device_ids=true | all-gather | bytes 573440 | tf_op jit(solution)/shard_map/all_gather | solution.py:173
  187.2 20.8 %collective-permute-start.6 = (bf16[4,8,7,8,128]{4,3,2,1,0:T(8,128)(2,1)S(1)}, bf16[4,8,7,8,128]{4,3,2,1,0:T(8,128)(2,1)S(1)}, u32[]{:S(2)}, u32[]{:S(2)}) collective-permute-start(bf16[4,8,7,8,128]{4,3,2,1,0:T(8,128)(2,1)S(1)} %bitcast.47), channel_id=1, source_target_pairs={{0,8},{8,0},{1,9},{9,1},{2,10},{10,2},{3,11},{11,3},{4,12},{12,4},... | collective-permute-start | bytes 1376264 | tf_op jit(solution)/shard_map/ppermute | solution.py:15
  208.0 1.9 collective-permute-start.5
  209.9 1.1 collective-permute-done.5
  212.1 1.3 convert_bitcast_fusion
  (45 shorter events, 5.7 us)
Async XLA Ops:
  0.6 1.5 copy-start
  3.4 18.3 %collective-permute-start = (bf16[288,128]{1,0:T(8,128)(2,1)S(1)}, bf16[288,128]{1,0:T(8,128)(2,1)S(1)}, u32[]{:S(2)}, u32[]{:S(2)}) collective-permute-start(bf16[288,128]{1,0:T(8,128)(2,1)S(1)} %pad_maximum_fusion.2), channel_id=1, source_target_pairs={{0,4},{4,0},{1,5},{5,1},{2,6},{6,2},{3,7},{7,3},{8,12},{12,8},{9,1... | collective-permute-start | bytes 221192 | tf_op jit(solution)/shard_map/ppermute | solution.py:15
  19.7 7.6 %collective-permute-start.2 = (bf16[288,128]{1,0:T(8,128)(2,1)S(1)}, bf16[288,128]{1,0:T(8,128)(2,1)S(1)}, u32[]{:S(2)}, u32[]{:S(2)}) collective-permute-start(bf16[288,128]{1,0:T(8,128)(2,1)S(1)} %pad_maximum_fusion.2), channel_id=1, source_target_pairs={{0,0},{1,16},{2,32},{3,48},{16,64},{17,80},{18,96},{19,112},{32,1}... | collective-permute-start | bytes 221192 | tf_op jit(solution)/shard_map/ppermute | solution.py:138
  21.7 7.6 %collective-permute-start.1 = (bf16[288,128]{1,0:T(8,128)(2,1)S(1)}, bf16[288,128]{1,0:T(8,128)(2,1)S(1)}, u32[]{:S(2)}, u32[]{:S(2)}) collective-permute-start(bf16[288,128]{1,0:T(8,128)(2,1)S(1)} %pad_maximum_fusion.4), channel_id=1, source_target_pairs={{0,8},{8,0},{1,9},{9,1},{2,10},{10,2},{3,11},{11,3},{4,12},{12,4},... | collective-permute-start | bytes 221192 | tf_op jit(solution)/shard_map/ppermute | solution.py:15
  27.3 3.1 %collective-permute-start.3 = (bf16[144,128]{1,0:T(8,128)(2,1)S(1)}, bf16[144,128]{1,0:T(8,128)(2,1)S(1)}, u32[]{:S(2)}, u32[]{:S(2)}) collective-permute-start(bf16[144,128]{1,0:T(8,128)(2,1)S(1)} %get-tuple-element.27), channel_id=1, source_target_pairs={{0,8},{8,0},{1,9},{9,1},{2,10},{10,2},{3,11},{11,3},{4,12},{12,4},... | collective-permute-start | bytes 110600 | tf_op jit(solution)/shard_map/ppermute | solution.py:15
  32.3 67.1 %all-to-all-start = ((bf16[16,576,128]{2,1,0:T(8,128)(2,1)}), bf16[16,576,128]{2,1,0:T(8,128)(2,1)S(1)}, u32[]{:S(2)}, u32[]{:S(2)}) async-start(bf16[16,576,128]{2,1,0:T(8,128)(2,1)} %broadcast_in_dim.6), calls=%async_computation | async-start | bytes 4718592 | tf_op jit(solution)/shard_map/all_to_all | solution.py:20
  99.4 1.1 copy-start.2
  106.8 1.1 copy-start.1
  107.9 6.9 %copy-start.3 = (bf16[128,1408]{1,0:T(8,128)(2,1)S(1)}, bf16[128,1408]{1,0:T(8,128)(2,1)}, u32[]{:S(2)}) copy-start(bf16[128,1408]{1,0:T(8,128)(2,1)} %param.7) | copy-start | bytes 1081348
  107.9 6.9 %copy-start.4 = (bf16[128,1408]{1,0:T(8,128)(2,1)S(1)}, bf16[128,1408]{1,0:T(8,128)(2,1)}, u32[]{:S(2)}) copy-start(bf16[128,1408]{1,0:T(8,128)(2,1)} %param.6) | copy-start | bytes 1081348
  107.9 22.5 %all-to-all-start.1 = ((bf16[16,160,256]{2,1,0:T(8,128)(2,1)}), bf16[16,160,256]{2,1,0:T(8,128)(2,1)S(1)}, u32[]{:S(2)}, u32[]{:S(2)}) async-start(bf16[16,160,256]{2,1,0:T(8,128)(2,1)} %copy-done.1), calls=%async_computation.1 | async-start | bytes 2621440 | tf_op jit(solution)/shard_map/all_to_all | solution.py:155
  114.8 15.5 %collective-permute-start.4 = (bf16[128,1408]{1,0:T(8,128)(2,1)S(1)}, bf16[128,1408]{1,0:T(8,128)(2,1)S(1)}, u32[]{:S(2)}, u32[]{:S(2)}) collective-permute-start(bf16[128,1408]{1,0:T(8,128)(2,1)S(1)} %broadcast_select_fusion.4), channel_id=1, source_target_pairs={{0,8},{8,0},{1,9},{9,1},{2,10},{10,2},{3,11},{11,3},{4,12},{12,4},... | collective-permute-start | bytes 1081352 | tf_op jit(solution)/shard_map/ppermute | solution.py:15
  131.9 13.5 %all-to-all-start.2 = ((f32[4,56,8,128]{3,2,1,0:T(8,128)}), f32[4,56,8,128]{3,2,1,0:T(8,128)S(1)}, u32[]{:S(2)}, u32[]{:S(2)}) async-start(f32[4,56,8,128]{3,2,1,0:T(8,128)} %bitcast.12), calls=%async_computation.2 | async-start | bytes 1835008 | tf_op jit(solution)/shard_map/all_to_all | solution.py:165
  187.2 24.7 %collective-permute-start.6 = (bf16[4,8,7,8,128]{4,3,2,1,0:T(8,128)(2,1)S(1)}, bf16[4,8,7,8,128]{4,3,2,1,0:T(8,128)(2,1)S(1)}, u32[]{:S(2)}, u32[]{:S(2)}) collective-permute-start(bf16[4,8,7,8,128]{4,3,2,1,0:T(8,128)(2,1)S(1)} %bitcast.47), channel_id=1, source_target_pairs={{0,8},{8,0},{1,9},{9,1},{2,10},{10,2},{3,11},{11,3},{4,12},{12,4},... | collective-permute-start | bytes 1376264 | tf_op jit(solution)/shard_map/ppermute | solution.py:15
  208.0 3.1 %collective-permute-start.5 = (f32[8,128]{1,0:T(8,128)S(1)}, f32[8,128]{1,0:T(8,128)S(1)}, u32[]{:S(2)}, u32[]{:S(2)}) collective-permute-start(f32[8,128]{1,0:T(8,128)S(1)} %slice_bitcast_fusion), channel_id=1, source_target_pairs={{0,8},{8,0},{1,9},{9,1},{2,10},{10,2},{3,11},{11,3},{4,12},{12,4},... | collective-permute-start | bytes 12296 | tf_op jit(solution)/shard_map/ppermute | solution.py:15

commit v3 on v2

--- a/solution.py
+++ b/solution.py
@@ -146,7 +146,9 @@
     ring_first, ring_second = ring[feats:], swap(ring[:feats], "core")
     plane = both_zh(mine, far[:feats])
     plane = jnp.concatenate([jnp.where(first, plane, beside), jnp.where(first, beside, plane)])
-    plane, ring_first, ring_second = lax.optimization_barrier((plane, ring_first, ring_second))
+    plane, ring_first, ring_second, pooled = lax.optimization_barrier(
+        (plane, ring_first, ring_second, pooled)
+    )
     plane = spread(plane, ("x", "y"), X * Y)
     ring_first = lax.all_gather(ring_first, ("zh", "zl"), axis=0, tiled=False)
     ring_second = lax.all_gather(ring_second, ("zh", "zl"), axis=0, tiled=False)
@@ -155,19 +157,19 @@
     parts = lax.all_to_all(parts, ("x", "y"), 0, 0, tiled=True)
     parts = jnp.sum(parts.astype(f32), axis=0)
     draw, tail = parts[:feats].astype(bf16), parts[feats : feats + 8, :128]
+    tail = jnp.where(first, tail, swap(tail, "core"))
 
     weight = jnp.dot(draw, pooled, preferred_element_type=f32)
 
     count = (feats // 8) * (width // 128)
     share = -(-count // (X * ZL))
-    tiles = weight.reshape(feats // 8, 8, width // 128, 128).transpose(0, 2, 1, 3)
+    tiles = weight.astype(bf16).reshape(feats // 8, 8, width // 128, 128).transpose(0, 2, 1, 3)
     tiles = jnp.pad(tiles.reshape(count, 8, 128), ((0, X * ZL * share - count), (0, 0), (0, 0)))
     tiles = lax.all_to_all(tiles.reshape(X, ZL * share, 8, 128), "x", 0, 0, tiled=True)
-    tiles = jnp.sum(tiles, axis=0).reshape(ZL, share, 8, 128)
+    tiles = jnp.sum(tiles.astype(f32), axis=0).reshape(ZL, share, 8, 128)
     tiles = jnp.concatenate([tiles, jnp.broadcast_to(tail, (ZL, 1, 8, 128))], axis=1)
     tiles = jnp.sum(lax.all_to_all(tiles, "zl", 0, 0, tiled=True), axis=0)
     tail = tiles[share]
-    tail = jnp.where(first, tail, swap(tail, "core"))
     sums = tail[0, :9].reshape(3, 3).sum(axis=1)
     tiles = spread(tiles[:share].astype(bf16), "zl", ZL)
     tiles = lax.all_gather(tiles, "x", axis=0, tiled=False)

time: 214 us -> 208 us (0.972)
  blocking collectives: 93.7 us -> 118 us
  starting transfers between devices: 86.3 us -> 68.5 us
  waiting for transfers between devices: 13.9 us -> 1.49 us
    all_to_all x0 -> x1, blocking collectives: none -> 19.2 us  [shards(): parts = lax.all_to_all(parts, ('x', 'y'), 0, 0, tiled=True)]
    ppermute x6, starting transfers between devices: 60.8 us -> 50.6 us  [swap(): return lax.ppermute(block, axis, [(0, 1), (1, 0)])]
    all_to_all x1, waiting for transfers between devices: 9.04 us -> 0.01 us  [shards(): lax.all_to_all(tiles.reshape(X, ZL * share, 8, 128), 'x', 0, 0, tiled=True)]
    all_to_all x1 -> x0, starting transfers between devices: 6.84 us -> none  [shards(): parts = lax.all_to_all(parts, ('x', 'y'), 0, 0, tiled=True)]
    all_gather x1, blocking collectives: 9.75 us -> 15.1 us  [shards(): tiles = lax.all_gather(tiles, 'x', axis=0, tiled=False)]
    ppermute x6, waiting for transfers between devices: 4.81 us -> 1.49 us  [swap(): return lax.ppermute(block, axis, [(0, 1), (1, 0)])]
  transfers between devices with their start and end apart: 10 -> 9, of which waited for: 5 -> 3; matrix products, arithmetic and copies ran while one was open for 1% -> 1% of each run, Pallas kernels for 0% -> 0%
where the time goes in v3:
time: 208 us; the launch traced here: 207 us
  blocking collectives  118 us (57%)
  starting transfers between devices  68.5 us (33%)
  Pallas kernels  6.34 us (3%)
  local copies, waits for them, and re-layouts  4.64 us (2%)
  matrix products  3.02 us (1%)
  other arithmetic  2.96 us (1%)
  between operations  2.28 us (1%)
    ppermute x6, starting transfers between devices, swap(): return lax.ppermute(block, axis, [(0, 1), (1, 0)])  50.6 us
    all_gather x1, blocking collectives, shards(): ring_first = lax.all_gather(ring_first, ('zh', 'zl'), axis=0, tiled=False)  26.3 us
    all_gather x1, blocking collectives, shards(): ring_second = lax.all_gather(ring_second, ('zh', 'zl'), axis=0, tiled=False)  25.7 us
    all_to_all x1, blocking collectives, shards(): parts = lax.all_to_all(parts, ('x', 'y'), 0, 0, tiled=True)  19.2 us
    all_to_all x1, blocking collectives, shards(): tiles = jnp.sum(lax.all_to_all(tiles, 'zl', 0, 0, tiled=True), axis=0)  17.3 us
    all_gather x1, blocking collectives, shards(): tiles = lax.all_gather(tiles, 'x', axis=0, tiled=False)  15.1 us
    all_to_all x1, blocking collectives, spread(): return lax.all_to_all(copies, axes, 0, 0, tiled=True)  14.6 us
    all_to_all x1, starting transfers between devices, spread(): return lax.all_to_all(copies, axes, 0, 0, tiled=True)  13.8 us
  transfers between devices with their start and end apart: 9, of which 3 were waited for; matrix products, arithmetic and copies ran while one was open for 1% of the time, Pallas kernels for 0%

profile of v3, /device:TPU:1, one launch (start us, length us, event | category | flops | bytes accessed | tf_op | source)
XLA Modules:
  0.0 207.5 jit_solution(14142057067065896878)
XLA Ops:
  0.7 1.5 convolution_convert_fusion.1
  2.2 1.3 broadcast_select_fusion.9
  3.5 16.3 %collective-permute-start = (bf16[288,128]{1,0:T(8,128)(2,1)S(1)}, bf16[288,128]{1,0:T(8,128)(2,1)S(1)}, u32[]{:S(2)}, u32[]{:S(2)}) collective-permute-start(bf16[288,128]{1,0:T(8,128)(2,1)S(1)} %pad_maximum_fusion.3), channel_id=1, source_target_pairs={{0,4},{4,0},{1,5},{5,1},{2,6},{6,2},{3,7},{7,3},{8,12},{12,8},{9,1... | collective-permute-start | bytes 221192 | tf_op jit(solution)/shard_map/ppermute | solution.py:15
  19.7 0.7 collective-permute-start.2
  20.5 2.9 %collective-permute-start.4 = (bf16[128,1408]{1,0:T(8,128)(2,1)S(1)}, bf16[128,1408]{1,0:T(8,128)(2,1)S(1)}, u32[]{:S(2)}, u32[]{:S(2)}) collective-permute-start(bf16[128,1408]{1,0:T(8,128)(2,1)S(1)} %broadcast_select_fusion.4), channel_id=1, source_target_pairs={{0,8},{8,0},{1,9},{9,1},{2,10},{10,2},{3,11},{11,3},{4,12},{12,4},... | collective-permute-start | bytes 1081352 | tf_op jit(solution)/shard_map/ppermute | solution.py:15
  23.4 3.9 %collective-permute-start.1 = (bf16[288,128]{1,0:T(8,128)(2,1)S(1)}, bf16[288,128]{1,0:T(8,128)(2,1)S(1)}, u32[]{:S(2)}, u32[]{:S(2)}) collective-permute-start(bf16[288,128]{1,0:T(8,128)(2,1)S(1)} %pad_maximum_fusion.5), channel_id=1, source_target_pairs={{0,8},{8,0},{1,9},{9,1},{2,10},{10,2},{3,11},{11,3},{4,12},{12,4},... | collective-permute-start | bytes 221192 | tf_op jit(solution)/shard_map/ppermute | solution.py:15
  27.4 1.9 collective-permute-start.3
  29.5 0.9 pad_maximum_fusion
  30.5 1.9 broadcast_in_dim.6
  32.3 13.8 %all-to-all-start = ((bf16[16,576,128]{2,1,0:T(8,128)(2,1)}), bf16[16,576,128]{2,1,0:T(8,128)(2,1)S(1)}, u32[]{:S(2)}, u32[]{:S(2)}) async-start(bf16[16,576,128]{2,1,0:T(8,128)(2,1)} %broadcast_in_dim.6), calls=%async_computation | async-start | bytes 4718592 | tf_op jit(solution)/shard_map/all_to_all | solution.py:20
  47.7 26.3 %all-gather = bf16[2304,128]{1,0:T(8,128)(2,1)S(1)} all-gather(bf16[144,128]{1,0:T(8,128)(2,1)S(1)} %get-tuple-element.13), channel_id=2, replica_groups=mesh['x'=4,'zl'=8,'core'=2,'zh'=2,'y'=4] {'zh','zl'}, dimensions={0}, use_global_device_ids=true | all-gather | bytes 626688 | tf_op jit(solution)/shard_map/all_gather | solution.py:153
  74.0 25.7 %all-gather.1 = bf16[2304,128]{1,0:T(8,128)(2,1)} all-gather(bf16[144,128]{1,0:T(8,128)(2,1)S(1)} %collective-permute-done.3), channel_id=3, replica_groups=mesh['x'=4,'zl'=8,'core'=2,'zh'=2,'y'=4] {'zh','zl'}, dimensions={0}, use_global_device_ids=true | all-gather | bytes 626688 | tf_op jit(solution)/shard_map/all_gather | solution.py:154
  99.7 1.1 copy-done.1
  100.8 6.3 %shard_map.101 = bf16[16,160,256]{2,1,0:T(8,128)(2,1)S(1)} custom-call(s32[5]{0:T(128)S(1)} %stack.32.place, f32[2]{0:T(128)S(1)} %pad_maximum_fusion.6.factors, bf16[16,576,128]{2,1,0:T(8,128)(2,1)S(1)} %all-to-all-done.plane, bf16[16,144,128]{2,1,0:T(8,128)(2,1)S(1)} %bitcast.43, bf16[16,144,128]{2,1,0:T(8,128)(2,1)S(1)} %bitcast.44), custom_call_target="tpu_custom_call" | custom-call | tf_op jit(solution)/shard_map/pallas_call | solution.py:104
  107.1 19.2 %all_to_all.25 = bf16[16,160,256]{2,1,0:T(8,128)(2,1)S(1)} all-to-all(bf16[16,160,256]{2,1,0:T(8,128)(2,1)S(1)} %shard_map.101), channel_id=1, replica_groups=mesh['x'=4,'zl'=8,'core'=2,'zh'=2,'y'=4] {'x','y'}, dimensions={0} | all-to-all | bytes 2621440 | tf_op jit(solution)/shard_map/all_to_all | solution.py:157
  126.8 0.8 pad.4
  127.6 3.5 %all-to-all-start.2 = ((bf16[4,56,8,128]{3,2,1,0:T(8,128)(2,1)}), bf16[4,56,8,128]{3,2,1,0:T(8,128)(2,1)S(1)}, u32[]{:S(2)}, u32[]{:S(2)}) async-start(bf16[4,56,8,128]{3,2,1,0:T(8,128)(2,1)} %bitcast.12), calls=%async_computation.2 | async-start | bytes 917504 | tf_op jit(solution)/shard_map/all_to_all | solution.py:168
  131.1 18.0 %collective-permute-start.5 = (f32[8,128]{1,0:T(8,128)S(1)}, f32[8,128]{1,0:T(8,128)S(1)}, u32[]{:S(2)}, u32[]{:S(2)}) collective-permute-start(f32[8,128]{1,0:T(8,128)S(1)} %slice.63), channel_id=1, source_target_pairs={{0,8},{8,0},{1,9},{9,1},{2,10},{10,2},{3,11},{11,3},{4,12},{12,4},... | collective-permute-start | bytes 12296 | tf_op jit(solution)/shard_map/ppermute | solution.py:15
  149.1 0.8 collective-permute-done.5
  150.0 17.3 %all_to_all.26 = f32[8,8,8,128]{3,2,1,0:T(8,128)S(1)} all-to-all(f32[8,8,8,128]{3,2,1,0:T(8,128)S(1)} %pad_maximum_fusion.1), channel_id=1, replica_groups=mesh['x'=4,'zl'=8,'core'=2,'zh'=2,'y'=4] {'zl'}, dimensions={0} | all-to-all | bytes 524288 | tf_op jit(solution)/shard_map/all_to_all | solution.py:171
  167.4 14.6 %all_to_all.27 = bf16[8,7,8,128]{3,2,1,0:T(8,128)(2,1)S(1)} all-to-all(bf16[8,7,8,128]{3,2,1,0:T(8,128)(2,1)S(1)} %broadcast_in_dim.8), channel_id=1, replica_groups=mesh['x'=4,'zl'=8,'core'=2,'zh'=2,'y'=4] {'zl'}, dimensions={0} | all-to-all | bytes 229376 | tf_op jit(solution)/shard_map/all_to_all | solution.py:20
  182.0 15.1 %all-gather.2 = bf16[32,7,8,128]{3,2,1,0:T(8,128)(2,1)S(1)} all-gather(bf16[8,7,8,128]{3,2,1,0:T(8,128)(2,1)S(1)} %all_to_all.27), channel_id=4, replica_groups=mesh['x'=4,'zl'=8,'core'=2,'zh'=2,'y'=4] {'x'}, dimensions={0}, use_global_device_ids=true | all-gather | bytes 573440 | tf_op jit(solution)/shard_map/all_gather | solution.py:175
  197.1 7.5 %collective-permute-start.6 = (bf16[4,8,7,8,128]{4,3,2,1,0:T(8,128)(2,1)S(1)}, bf16[4,8,7,8,128]{4,3,2,1,0:T(8,128)(2,1)S(1)}, u32[]{:S(2)}, u32[]{:S(2)}) collective-permute-start(bf16[4,8,7,8,128]{4,3,2,1,0:T(8,128)(2,1)S(1)} %bitcast.45), channel_id=1, source_target_pairs={{0,8},{8,0},{1,9},{9,1},{2,10},{10,2},{3,11},{11,3},{4,12},{12,4},... | collective-permute-start | bytes 1376264 | tf_op jit(solution)/shard_map/ppermute | solution.py:15
  206.2 1.3 convert_bitcast_fusion
  (45 shorter events, 2.6 us)
Async XLA Ops:
  0.6 1.5 copy-start
  0.6 19.8 %copy-start.2 = (bf16[128,1408]{1,0:T(8,128)(2,1)S(1)}, bf16[128,1408]{1,0:T(8,128)(2,1)}, u32[]{:S(2)}) copy-start(bf16[128,1408]{1,0:T(8,128)(2,1)} %param.7) | copy-start | bytes 1081348
  0.7 19.8 %copy-start.3 = (bf16[128,1408]{1,0:T(8,128)(2,1)S(1)}, bf16[128,1408]{1,0:T(8,128)(2,1)}, u32[]{:S(2)}) copy-start(bf16[128,1408]{1,0:T(8,128)(2,1)} %param.6) | copy-start | bytes 1081348
  3.5 19.9 %collective-permute-start = (bf16[288,128]{1,0:T(8,128)(2,1)S(1)}, bf16[288,128]{1,0:T(8,128)(2,1)S(1)}, u32[]{:S(2)}, u32[]{:S(2)}) collective-permute-start(bf16[288,128]{1,0:T(8,128)(2,1)S(1)} %pad_maximum_fusion.3), channel_id=1, source_target_pairs={{0,4},{4,0},{1,5},{5,1},{2,6},{6,2},{3,7},{7,3},{8,12},{12,8},{9,1... | collective-permute-start | bytes 221192 | tf_op jit(solution)/shard_map/ppermute | solution.py:15
  19.7 7.6 %collective-permute-start.2 = (bf16[288,128]{1,0:T(8,128)(2,1)S(1)}, bf16[288,128]{1,0:T(8,128)(2,1)S(1)}, u32[]{:S(2)}, u32[]{:S(2)}) collective-permute-start(bf16[288,128]{1,0:T(8,128)(2,1)S(1)} %pad_maximum_fusion.3), channel_id=1, source_target_pairs={{0,0},{1,16},{2,32},{3,48},{16,64},{17,80},{18,96},{19,112},{32,1}... | collective-permute-start | bytes 221192 | tf_op jit(solution)/shard_map/ppermute | solution.py:138
  20.5 8.9 %collective-permute-start.4 = (bf16[128,1408]{1,0:T(8,128)(2,1)S(1)}, bf16[128,1408]{1,0:T(8,128)(2,1)S(1)}, u32[]{:S(2)}, u32[]{:S(2)}) collective-permute-start(bf16[128,1408]{1,0:T(8,128)(2,1)S(1)} %broadcast_select_fusion.4), channel_id=1, source_target_pairs={{0,8},{8,0},{1,9},{9,1},{2,10},{10,2},{3,11},{11,3},{4,12},{12,4},... | collective-permute-start | bytes 1081352 | tf_op jit(solution)/shard_map/ppermute | solution.py:15
  23.4 5.9 %collective-permute-start.1 = (bf16[288,128]{1,0:T(8,128)(2,1)S(1)}, bf16[288,128]{1,0:T(8,128)(2,1)S(1)}, u32[]{:S(2)}, u32[]{:S(2)}) collective-permute-start(bf16[288,128]{1,0:T(8,128)(2,1)S(1)} %pad_maximum_fusion.5), channel_id=1, source_target_pairs={{0,8},{8,0},{1,9},{9,1},{2,10},{10,2},{3,11},{11,3},{4,12},{12,4},... | collective-permute-start | bytes 221192 | tf_op jit(solution)/shard_map/ppermute | solution.py:15
  27.4 3.1 %collective-permute-start.3 = (bf16[144,128]{1,0:T(8,128)(2,1)S(1)}, bf16[144,128]{1,0:T(8,128)(2,1)S(1)}, u32[]{:S(2)}, u32[]{:S(2)}) collective-permute-start(bf16[144,128]{1,0:T(8,128)(2,1)S(1)} %get-tuple-element.29), channel_id=1, source_target_pairs={{0,8},{8,0},{1,9},{9,1},{2,10},{10,2},{3,11},{11,3},{4,12},{12,4},... | collective-permute-start | bytes 110600 | tf_op jit(solution)/shard_map/ppermute | solution.py:15
  32.3 67.4 %all-to-all-start = ((bf16[16,576,128]{2,1,0:T(8,128)(2,1)}), bf16[16,576,128]{2,1,0:T(8,128)(2,1)S(1)}, u32[]{:S(2)}, u32[]{:S(2)}) async-start(bf16[16,576,128]{2,1,0:T(8,128)(2,1)} %broadcast_in_dim.6), calls=%async_computation | async-start | bytes 4718592 | tf_op jit(solution)/shard_map/all_to_all | solution.py:20
  99.7 1.1 copy-start.1
  107.1 19.4 %copy-start.4 = (bf16[256,1408]{1,0:T(8,128)(2,1)S(1)}, bf16[256,1408]{1,0:T(8,128)(2,1)}, u32[]{:S(2)}) copy-start(bf16[256,1408]{1,0:T(8,128)(2,1)} %pad_maximum_fusion) | copy-start | bytes 2162692
  127.6 22.3 %all-to-all-start.2 = ((bf16[4,56,8,128]{3,2,1,0:T(8,128)(2,1)}), bf16[4,56,8,128]{3,2,1,0:T(8,128)(2,1)S(1)}, u32[]{:S(2)}, u32[]{:S(2)}) async-start(bf16[4,56,8,128]{3,2,1,0:T(8,128)(2,1)} %bitcast.12), calls=%async_computation.2 | async-start | bytes 917504 | tf_op jit(solution)/shard_map/all_to_all | solution.py:168
  131.1 18.8 %collective-permute-start.5 = (f32[8,128]{1,0:T(8,128)S(1)}, f32[8,128]{1,0:T(8,128)S(1)}, u32[]{:S(2)}, u32[]{:S(2)}) collective-permute-start(f32[8,128]{1,0:T(8,128)S(1)} %slice.63), channel_id=1, source_target_pairs={{0,8},{8,0},{1,9},{9,1},{2,10},{10,2},{3,11},{11,3},{4,12},{12,4},... | collective-permute-start | bytes 12296 | tf_op jit(solution)/shard_map/ppermute | solution.py:15
  197.1 9.0 %collective-permute-start.6 = (bf16[4,8,7,8,128]{4,3,2,1,0:T(8,128)(2,1)S(1)}, bf16[4,8,7,8,128]{4,3,2,1,0:T(8,128)(2,1)S(1)}, u32[]{:S(2)}, u32[]{:S(2)}) collective-permute-start(bf16[4,8,7,8,128]{4,3,2,1,0:T(8,128)(2,1)S(1)} %bitcast.45), channel_id=1, source_target_pairs={{0,8},{8,0},{1,9},{9,1},{2,10},{10,2},{3,11},{11,3},{4,12},{12,4},... | collective-permute-start | bytes 1376264 | tf_op jit(solution)/shard_map/ppermute | solution.py:15

commit v4 on v3

--- a/solution.py
+++ b/solution.py
@@ -55,17 +55,18 @@
     own_at = pl.multiple_of(zh * own, 16)
     ring_own = ring_raw[pl.ds(own_at, own), :]
 
-    lane = lax.broadcasted_iota(jnp.int32, (rows, block), 1)
-    row = lax.broadcasted_iota(jnp.int32, (rows, block), 0)
+    pair = CORE * rows
+    lane = lax.broadcasted_iota(jnp.int32, (pair, block), 1)
+    row = lax.broadcasted_iota(jnp.int32, (pair, block), 0)
     ring_id = ((x * ZL + 2 * y) * CORE + lane // rows) * rows + lane % rows
     loss = grad_scale = grad_bias = jnp.zeros((1, block), f32)
-    for a in range(X * CORE):
-        images = plane_raw[:, pl.ds(a * rows, rows)].T
+    for a in range(X):
+        images = plane_raw[:, pl.ds(a * pair, pair)].T
         wide = images.astype(f32)
         inv = 1.0 / jnp.sqrt(jnp.sum(wide * wide, axis=1, keepdims=True) + eps)
         dots = jnp.dot(images, ring_raw[...], preferred_element_type=f32) * inv * ring_inv
         logits = scale * dots + bias
-        plane_id = ((a // CORE * ZL + zl) * CORE + a % CORE) * rows + row
+        plane_id = (a * ZL + zl) * pair + row
         label = jnp.where(plane_id == ring_id, f32(1.0), f32(-1.0))
         margin = label * logits
         small = jnp.exp(-jnp.abs(margin))
@@ -76,17 +77,17 @@
         grad_scale += jnp.sum(inner, axis=0, keepdims=True)
         grad_bias += jnp.sum(pair_grad, axis=0, keepdims=True)
         shift = scale * jnp.sum(inner, axis=1, keepdims=True) * inv
-        shift = jnp.broadcast_to(shift, (rows, rows)).T[:1]
-        inv = jnp.broadcast_to(inv, (rows, rows)).T[:1]
+        shift = jnp.broadcast_to(shift, (pair, rows)).T[:1]
+        inv = jnp.broadcast_to(inv, (pair, rows)).T[:1]
         coef = (scale * pair_grad * ring_inv).astype(bf16)
         draw = lax.dot_general(
             ring_own, coef, (((1,), (1,)), ((), ())), preferred_element_type=f32
         )
-        raw = plane_raw[pl.ds(own_at, own), pl.ds(a * rows, rows)].astype(f32)
+        raw = plane_raw[pl.ds(own_at, own), pl.ds(a * pair, pair)].astype(f32)
         draw = ((draw - raw * shift) * inv).astype(bf16)
         for b in range(Y):
             part = draw[b * feats : (b + 1) * feats]
-            out[a // CORE * Y + b, pl.ds(0, feats), pl.ds(a % CORE * rows, rows)] = part
+            out[a * Y + b, pl.ds(0, feats), :] = part
 
     lane = lax.broadcasted_iota(jnp.int32, (TAIL, CORE * rows), 1)
     tail = jnp.zeros((TAIL, CORE * rows), f32)

time: 208 us -> 208 us (level)
  no operation moved by 1% of the time
where the time goes in v4:
time: 208 us; the launch traced here: 207 us
  blocking collectives  118 us (57%)
  starting transfers between devices  68.5 us (33%)
  Pallas kernels  5.99 us (3%)
  local copies, waits for them, and re-layouts  4.64 us (2%)
  matrix products  3.02 us (1%)
  other arithmetic  2.96 us (1%)
  between operations  2.29 us (1%)
    ppermute x6, starting transfers between devices, swap(): return lax.ppermute(block, axis, [(0, 1), (1, 0)])  50.6 us
    all_gather x1, blocking collectives, shards(): ring_first = lax.all_gather(ring_first, ('zh', 'zl'), axis=0, tiled=False)  26.3 us
    all_gather x1, blocking collectives, shards(): ring_second = lax.all_gather(ring_second, ('zh', 'zl'), axis=0, tiled=False)  25.7 us
    all_to_all x1, blocking collectives, shards(): parts = lax.all_to_all(parts, ('x', 'y'), 0, 0, tiled=True)  19.2 us
    all_to_all x1, blocking collectives, shards(): tiles = jnp.sum(lax.all_to_all(tiles, 'zl', 0, 0, tiled=True), axis=0)  17.3 us
    all_gather x1, blocking collectives, shards(): tiles = lax.all_gather(tiles, 'x', axis=0, tiled=False)  15.1 us
    all_to_all x1, blocking collectives, spread(): return lax.all_to_all(copies, axes, 0, 0, tiled=True)  14.6 us
    all_to_all x1, starting transfers between devices, spread(): return lax.all_to_all(copies, axes, 0, 0, tiled=True)  13.8 us
  transfers between devices with their start and end apart: 9, of which 3 were waited for; matrix products, arithmetic and copies ran while one was open for 1% of the time, Pallas kernels for 0%

profile of v4, /device:TPU:1, one launch (start us, length us, event | category | flops | bytes accessed | tf_op | source)
XLA Modules:
  0.0 207.1 jit_solution(8232457059288678990)
XLA Ops:
  0.7 1.5 convolution_convert_fusion.1
  2.2 1.3 broadcast_select_fusion.9
  3.5 16.3 %collective-permute-start = (bf16[288,128]{1,0:T(8,128)(2,1)S(1)}, bf16[288,128]{1,0:T(8,128)(2,1)S(1)}, u32[]{:S(2)}, u32[]{:S(2)}) collective-permute-start(bf16[288,128]{1,0:T(8,128)(2,1)S(1)} %pad_maximum_fusion.3), channel_id=1, source_target_pairs={{0,4},{4,0},{1,5},{5,1},{2,6},{6,2},{3,7},{7,3},{8,12},{12,8},{9,1... | collective-permute-start | bytes 221192 | tf_op jit(solution)/shard_map/ppermute | solution.py:15
  19.7 0.7 collective-permute-start.2
  20.5 2.9 %collective-permute-start.4 = (bf16[128,1408]{1,0:T(8,128)(2,1)S(1)}, bf16[128,1408]{1,0:T(8,128)(2,1)S(1)}, u32[]{:S(2)}, u32[]{:S(2)}) collective-permute-start(bf16[128,1408]{1,0:T(8,128)(2,1)S(1)} %broadcast_select_fusion.4), channel_id=1, source_target_pairs={{0,8},{8,0},{1,9},{9,1},{2,10},{10,2},{3,11},{11,3},{4,12},{12,4},... | collective-permute-start | bytes 1081352 | tf_op jit(solution)/shard_map/ppermute | solution.py:15
  23.4 3.9 %collective-permute-start.1 = (bf16[288,128]{1,0:T(8,128)(2,1)S(1)}, bf16[288,128]{1,0:T(8,128)(2,1)S(1)}, u32[]{:S(2)}, u32[]{:S(2)}) collective-permute-start(bf16[288,128]{1,0:T(8,128)(2,1)S(1)} %pad_maximum_fusion.5), channel_id=1, source_target_pairs={{0,8},{8,0},{1,9},{9,1},{2,10},{10,2},{3,11},{11,3},{4,12},{12,4},... | collective-permute-start | bytes 221192 | tf_op jit(solution)/shard_map/ppermute | solution.py:15
  27.4 1.9 collective-permute-start.3
  29.5 0.9 pad_maximum_fusion
  30.5 1.9 broadcast_in_dim.6
  32.3 13.8 %all-to-all-start = ((bf16[16,576,128]{2,1,0:T(8,128)(2,1)}), bf16[16,576,128]{2,1,0:T(8,128)(2,1)S(1)}, u32[]{:S(2)}, u32[]{:S(2)}) async-start(bf16[16,576,128]{2,1,0:T(8,128)(2,1)} %broadcast_in_dim.6), calls=%async_computation | async-start | bytes 4718592 | tf_op jit(solution)/shard_map/all_to_all | solution.py:20
  47.7 26.3 %all-gather = bf16[2304,128]{1,0:T(8,128)(2,1)S(1)} all-gather(bf16[144,128]{1,0:T(8,128)(2,1)S(1)} %get-tuple-element.13), channel_id=2, replica_groups=mesh['x'=4,'zl'=8,'core'=2,'zh'=2,'y'=4] {'zh','zl'}, dimensions={0}, use_global_device_ids=true | all-gather | bytes 626688 | tf_op jit(solution)/shard_map/all_gather | solution.py:154
  74.0 25.7 %all-gather.1 = bf16[2304,128]{1,0:T(8,128)(2,1)} all-gather(bf16[144,128]{1,0:T(8,128)(2,1)S(1)} %collective-permute-done.3), channel_id=3, replica_groups=mesh['x'=4,'zl'=8,'core'=2,'zh'=2,'y'=4] {'zh','zl'}, dimensions={0}, use_global_device_ids=true | all-gather | bytes 626688 | tf_op jit(solution)/shard_map/all_gather | solution.py:155
  99.7 1.1 copy-done.1
  100.8 6.0 %shard_map.101 = bf16[16,160,256]{2,1,0:T(8,128)(2,1)S(1)} custom-call(s32[5]{0:T(128)S(1)} %stack.32.place, f32[2]{0:T(128)S(1)} %pad_maximum_fusion.6.factors, bf16[16,576,128]{2,1,0:T(8,128)(2,1)S(1)} %all-to-all-done.plane, bf16[16,144,128]{2,1,0:T(8,128)(2,1)S(1)} %bitcast.43, bf16[16,144,128]{2,1,0:T(8,128)(2,1)S(1)} %bitcast.44), custom_call_target="tpu_custom_call" | custom-call | tf_op jit(solution)/shard_map/pallas_call | solution.py:105
  106.8 19.2 %all_to_all.25 = bf16[16,160,256]{2,1,0:T(8,128)(2,1)S(1)} all-to-all(bf16[16,160,256]{2,1,0:T(8,128)(2,1)S(1)} %shard_map.101), channel_id=1, replica_groups=mesh['x'=4,'zl'=8,'core'=2,'zh'=2,'y'=4] {'x','y'}, dimensions={0} | all-to-all | bytes 2621440 | tf_op jit(solution)/shard_map/all_to_all | solution.py:158
  126.4 0.8 pad.4
  127.2 3.5 %all-to-all-start.2 = ((bf16[4,56,8,128]{3,2,1,0:T(8,128)(2,1)}), bf16[4,56,8,128]{3,2,1,0:T(8,128)(2,1)S(1)}, u32[]{:S(2)}, u32[]{:S(2)}) async-start(bf16[4,56,8,128]{3,2,1,0:T(8,128)(2,1)} %bitcast.12), calls=%async_computation.2 | async-start | bytes 917504 | tf_op jit(solution)/shard_map/all_to_all | solution.py:169
  130.7 18.0 %collective-permute-start.5 = (f32[8,128]{1,0:T(8,128)S(1)}, f32[8,128]{1,0:T(8,128)S(1)}, u32[]{:S(2)}, u32[]{:S(2)}) collective-permute-start(f32[8,128]{1,0:T(8,128)S(1)} %slice.63), channel_id=1, source_target_pairs={{0,8},{8,0},{1,9},{9,1},{2,10},{10,2},{3,11},{11,3},{4,12},{12,4},... | collective-permute-start | bytes 12296 | tf_op jit(solution)/shard_map/ppermute | solution.py:15
  148.8 0.8 collective-permute-done.5
  149.7 17.3 %all_to_all.26 = f32[8,8,8,128]{3,2,1,0:T(8,128)S(1)} all-to-all(f32[8,8,8,128]{3,2,1,0:T(8,128)S(1)} %pad_maximum_fusion.1), channel_id=1, replica_groups=mesh['x'=4,'zl'=8,'core'=2,'zh'=2,'y'=4] {'zl'}, dimensions={0} | all-to-all | bytes 524288 | tf_op jit(solution)/shard_map/all_to_all | solution.py:172
  167.1 14.6 %all_to_all.27 = bf16[8,7,8,128]{3,2,1,0:T(8,128)(2,1)S(1)} all-to-all(bf16[8,7,8,128]{3,2,1,0:T(8,128)(2,1)S(1)} %broadcast_in_dim.8), channel_id=1, replica_groups=mesh['x'=4,'zl'=8,'core'=2,'zh'=2,'y'=4] {'zl'}, dimensions={0} | all-to-all | bytes 229376 | tf_op jit(solution)/shard_map/all_to_all | solution.py:20
  181.7 15.1 %all-gather.2 = bf16[32,7,8,128]{3,2,1,0:T(8,128)(2,1)S(1)} all-gather(bf16[8,7,8,128]{3,2,1,0:T(8,128)(2,1)S(1)} %all_to_all.27), channel_id=4, replica_groups=mesh['x'=4,'zl'=8,'core'=2,'zh'=2,'y'=4] {'x'}, dimensions={0}, use_global_device_ids=true | all-gather | bytes 573440 | tf_op jit(solution)/shard_map/all_gather | solution.py:176
  196.7 7.5 %collective-permute-start.6 = (bf16[4,8,7,8,128]{4,3,2,1,0:T(8,128)(2,1)S(1)}, bf16[4,8,7,8,128]{4,3,2,1,0:T(8,128)(2,1)S(1)}, u32[]{:S(2)}, u32[]{:S(2)}) collective-permute-start(bf16[4,8,7,8,128]{4,3,2,1,0:T(8,128)(2,1)S(1)} %bitcast.45), channel_id=1, source_target_pairs={{0,8},{8,0},{1,9},{9,1},{2,10},{10,2},{3,11},{11,3},{4,12},{12,4},... | collective-permute-start | bytes 1376264 | tf_op jit(solution)/shard_map/ppermute | solution.py:15
  205.8 1.3 convert_bitcast_fusion
  (45 shorter events, 2.6 us)
Async XLA Ops:
  0.6 1.5 copy-start
  0.6 19.8 %copy-start.2 = (bf16[128,1408]{1,0:T(8,128)(2,1)S(1)}, bf16[128,1408]{1,0:T(8,128)(2,1)}, u32[]{:S(2)}) copy-start(bf16[128,1408]{1,0:T(8,128)(2,1)} %param.7) | copy-start | bytes 1081348
  0.7 19.8 %copy-start.3 = (bf16[128,1408]{1,0:T(8,128)(2,1)S(1)}, bf16[128,1408]{1,0:T(8,128)(2,1)}, u32[]{:S(2)}) copy-start(bf16[128,1408]{1,0:T(8,128)(2,1)} %param.6) | copy-start | bytes 1081348
  3.5 19.9 %collective-permute-start = (bf16[288,128]{1,0:T(8,128)(2,1)S(1)}, bf16[288,128]{1,0:T(8,128)(2,1)S(1)}, u32[]{:S(2)}, u32[]{:S(2)}) collective-permute-start(bf16[288,128]{1,0:T(8,128)(2,1)S(1)} %pad_maximum_fusion.3), channel_id=1, source_target_pairs={{0,4},{4,0},{1,5},{5,1},{2,6},{6,2},{3,7},{7,3},{8,12},{12,8},{9,1... | collective-permute-start | bytes 221192 | tf_op jit(solution)/shard_map/ppermute | solution.py:15
  19.7 7.6 %collective-permute-start.2 = (bf16[288,128]{1,0:T(8,128)(2,1)S(1)}, bf16[288,128]{1,0:T(8,128)(2,1)S(1)}, u32[]{:S(2)}, u32[]{:S(2)}) collective-permute-start(bf16[288,128]{1,0:T(8,128)(2,1)S(1)} %pad_maximum_fusion.3), channel_id=1, source_target_pairs={{0,0},{1,16},{2,32},{3,48},{16,64},{17,80},{18,96},{19,112},{32,1}... | collective-permute-start | bytes 221192 | tf_op jit(solution)/shard_map/ppermute | solution.py:139
  20.5 8.9 %collective-permute-start.4 = (bf16[128,1408]{1,0:T(8,128)(2,1)S(1)}, bf16[128,1408]{1,0:T(8,128)(2,1)S(1)}, u32[]{:S(2)}, u32[]{:S(2)}) collective-permute-start(bf16[128,1408]{1,0:T(8,128)(2,1)S(1)} %broadcast_select_fusion.4), channel_id=1, source_target_pairs={{0,8},{8,0},{1,9},{9,1},{2,10},{10,2},{3,11},{11,3},{4,12},{12,4},... | collective-permute-start | bytes 1081352 | tf_op jit(solution)/shard_map/ppermute | solution.py:15
  23.4 5.9 %collective-permute-start.1 = (bf16[288,128]{1,0:T(8,128)(2,1)S(1)}, bf16[288,128]{1,0:T(8,128)(2,1)S(1)}, u32[]{:S(2)}, u32[]{:S(2)}) collective-permute-start(bf16[288,128]{1,0:T(8,128)(2,1)S(1)} %pad_maximum_fusion.5), channel_id=1, source_target_pairs={{0,8},{8,0},{1,9},{9,1},{2,10},{10,2},{3,11},{11,3},{4,12},{12,4},... | collective-permute-start | bytes 221192 | tf_op jit(solution)/shard_map/ppermute | solution.py:15
  27.4 3.1 %collective-permute-start.3 = (bf16[144,128]{1,0:T(8,128)(2,1)S(1)}, bf16[144,128]{1,0:T(8,128)(2,1)S(1)}, u32[]{:S(2)}, u32[]{:S(2)}) collective-permute-start(bf16[144,128]{1,0:T(8,128)(2,1)S(1)} %get-tuple-element.29), channel_id=1, source_target_pairs={{0,8},{8,0},{1,9},{9,1},{2,10},{10,2},{3,11},{11,3},{4,12},{12,4},... | collective-permute-start | bytes 110600 | tf_op jit(solution)/shard_map/ppermute | solution.py:15
  32.3 67.4 %all-to-all-start = ((bf16[16,576,128]{2,1,0:T(8,128)(2,1)}), bf16[16,576,128]{2,1,0:T(8,128)(2,1)S(1)}, u32[]{:S(2)}, u32[]{:S(2)}) async-start(bf16[16,576,128]{2,1,0:T(8,128)(2,1)} %broadcast_in_dim.6), calls=%async_computation | async-start | bytes 4718592 | tf_op jit(solution)/shard_map/all_to_all | solution.py:20
  99.7 1.1 copy-start.1
  106.8 19.4 %copy-start.4 = (bf16[256,1408]{1,0:T(8,128)(2,1)S(1)}, bf16[256,1408]{1,0:T(8,128)(2,1)}, u32[]{:S(2)}) copy-start(bf16[256,1408]{1,0:T(8,128)(2,1)} %pad_maximum_fusion) | copy-start | bytes 2162692
  127.2 22.3 %all-to-all-start.2 = ((bf16[4,56,8,128]{3,2,1,0:T(8,128)(2,1)}), bf16[4,56,8,128]{3,2,1,0:T(8,128)(2,1)S(1)}, u32[]{:S(2)}, u32[]{:S(2)}) async-start(bf16[4,56,8,128]{3,2,1,0:T(8,128)(2,1)} %bitcast.12), calls=%async_computation.2 | async-start | bytes 917504 | tf_op jit(solution)/shard_map/all_to_all | solution.py:169
  130.7 18.9 %collective-permute-start.5 = (f32[8,128]{1,0:T(8,128)S(1)}, f32[8,128]{1,0:T(8,128)S(1)}, u32[]{:S(2)}, u32[]{:S(2)}) collective-permute-start(f32[8,128]{1,0:T(8,128)S(1)} %slice.63), channel_id=1, source_target_pairs={{0,8},{8,0},{1,9},{9,1},{2,10},{10,2},{3,11},{11,3},{4,12},{12,4},... | collective-permute-start | bytes 12296 | tf_op jit(solution)/shard_map/ppermute | solution.py:15
  196.7 9.0 %collective-permute-start.6 = (bf16[4,8,7,8,128]{4,3,2,1,0:T(8,128)(2,1)S(1)}, bf16[4,8,7,8,128]{4,3,2,1,0:T(8,128)(2,1)S(1)}, u32[]{:S(2)}, u32[]{:S(2)}) collective-permute-start(bf16[4,8,7,8,128]{4,3,2,1,0:T(8,128)(2,1)S(1)} %bitcast.45), channel_id=1, source_target_pairs={{0,8},{8,0},{1,9},{9,1},{2,10},{10,2},{3,11},{11,3},{4,12},{12,4},... | collective-permute-start | bytes 1376264 | tf_op jit(solution)/shard_map/ppermute | solution.py:15

commit v5 on v4

--- a/solution.py
+++ b/solution.py
@@ -39,11 +39,12 @@
     total = rows * X * ZL * CORE
 
     for s in range(X * Y):
-        for g in range(CORE):
-            lanes = pl.ds((s // Y * CORE + g) * rows, rows)
-            for h in range(ZH):
+        for g, owner in enumerate((core, 1 - core)):
+            lanes = pl.ds(pl.multiple_of((s // Y * CORE + owner) * rows, rows), rows)
+            for h, half in enumerate((zh, 1 - zh)):
+                at = pl.multiple_of((half * Y + s % Y) * feats, 16)
                 piece = plane[s, pl.ds((g * ZH + h) * feats, feats), :]
-                plane_raw[pl.ds((h * Y + s % Y) * feats, feats), lanes] = piece
+                plane_raw[pl.ds(at, feats), lanes] = piece
     for ref, owner in ((ring_mine, core), (ring_other, 1 - core)):
         for s in range(ZH * ZL):
             at = (s // ZL * Y + s % Y) * feats
@@ -138,15 +139,9 @@
     raw = jnp.concatenate([mine, theirs])
     ring = lax.ppermute(raw, ("zl", "y"), to_ring)
     far = swap(raw, "zh")
-    low = zh == 0
-
-    def both_zh(here, there):
-        return jnp.concatenate([jnp.where(low, here, there), jnp.where(low, there, here)])
-
-    beside = swap(both_zh(theirs, far[feats:]), "core")
+    beside = swap(jnp.concatenate([theirs, far[feats:]]), "core")
     ring_first, ring_second = ring[feats:], swap(ring[:feats], "core")
-    plane = both_zh(mine, far[:feats])
-    plane = jnp.concatenate([jnp.where(first, plane, beside), jnp.where(first, beside, plane)])
+    plane = jnp.concatenate([mine, far[:feats], beside])
     plane, ring_first, ring_second, pooled = lax.optimization_barrier(
         (plane, ring_first, ring_second, pooled)
     )

time: 208 us -> 208 us (level)
  no operation moved by 1% of the time
where the time goes in v5:
time: 208 us
  blocking collectives  118 us (57%)
  starting transfers between devices  68.5 us (33%)
  Pallas kernels  6.44 us (3%)
  local copies, waits for them, and re-layouts  4.66 us (2%)
  matrix products  3.02 us (1%)
  other arithmetic  2.9 us (1%)
  between operations  2.28 us (1%)
    ppermute x6, starting transfers between devices, swap(): return lax.ppermute(block, axis, [(0, 1), (1, 0)])  50.6 us
    all_gather x1, blocking collectives, shards(): ring_first = lax.all_gather(ring_first, ('zh', 'zl'), axis=0, tiled=False)  26.3 us
    all_gather x1, blocking collectives, shards(): ring_second = lax.all_gather(ring_second, ('zh', 'zl'), axis=0, tiled=False)  25.8 us
    all_to_all x1, blocking collectives, shards(): parts = lax.all_to_all(parts, ('x', 'y'), 0, 0, tiled=True)  19 us
    all_to_all x1, blocking collectives, shards(): tiles = jnp.sum(lax.all_to_all(tiles, 'zl', 0, 0, tiled=True), axis=0)  17.4 us
    all_gather x1, blocking collectives, shards(): tiles = lax.all_gather(tiles, 'x', axis=0, tiled=False)  15.1 us
    all_to_all x1, blocking collectives, spread(): return lax.all_to_all(copies, axes, 0, 0, tiled=True)  14.6 us
    all_to_all x1, starting transfers between devices, spread(): return lax.all_to_all(copies, axes, 0, 0, tiled=True)  13.8 us
  transfers between devices with their start and end apart: 9, of which 3 were waited for; matrix products, arithmetic and copies ran while one was open for 1% of the time, Pallas kernels for 0%

profile of v5, /device:TPU:1, one launch (start us, length us, event | category | flops | bytes accessed | tf_op | source)
XLA Modules:
  0.0 207.6 jit_solution(7598847692143803204)
XLA Ops:
  0.7 1.5 convolution_convert_fusion.1
  2.2 1.3 broadcast_select_fusion.7
  3.5 16.3 %collective-permute-start = (bf16[288,128]{1,0:T(8,128)(2,1)S(1)}, bf16[288,128]{1,0:T(8,128)(2,1)S(1)}, u32[]{:S(2)}, u32[]{:S(2)}) collective-permute-start(bf16[288,128]{1,0:T(8,128)(2,1)S(1)} %pad_maximum_fusion.3), channel_id=1, source_target_pairs={{0,4},{4,0},{1,5},{5,1},{2,6},{6,2},{3,7},{7,3},{8,12},{12,8},{9,1... | collective-permute-start | bytes 221192 | tf_op jit(solution)/shard_map/ppermute | solution.py:15
  19.7 0.7 collective-permute-start.2
  20.5 2.9 %collective-permute-start.4 = (bf16[128,1408]{1,0:T(8,128)(2,1)S(1)}, bf16[128,1408]{1,0:T(8,128)(2,1)S(1)}, u32[]{:S(2)}, u32[]{:S(2)}) collective-permute-start(bf16[128,1408]{1,0:T(8,128)(2,1)S(1)} %broadcast_select_fusion.4), channel_id=1, source_target_pairs={{0,8},{8,0},{1,9},{9,1},{2,10},{10,2},{3,11},{11,3},{4,12},{12,4},... | collective-permute-start | bytes 1081352 | tf_op jit(solution)/shard_map/ppermute | solution.py:15
  23.4 3.9 %collective-permute-start.1 = (bf16[288,128]{1,0:T(8,128)(2,1)S(1)}, bf16[288,128]{1,0:T(8,128)(2,1)S(1)}, u32[]{:S(2)}, u32[]{:S(2)}) collective-permute-start(bf16[288,128]{1,0:T(8,128)(2,1)S(1)} %pad_maximum_fusion.4), channel_id=1, source_target_pairs={{0,8},{8,0},{1,9},{9,1},{2,10},{10,2},{3,11},{11,3},{4,12},{12,4},... | collective-permute-start | bytes 221192 | tf_op jit(solution)/shard_map/ppermute | solution.py:15
  27.4 1.9 collective-permute-start.3
  29.4 0.9 pad_maximum_fusion
  30.5 1.9 broadcast_in_dim.6
  32.3 13.8 %all-to-all-start = ((bf16[16,576,128]{2,1,0:T(8,128)(2,1)}), bf16[16,576,128]{2,1,0:T(8,128)(2,1)S(1)}, u32[]{:S(2)}, u32[]{:S(2)}) async-start(bf16[16,576,128]{2,1,0:T(8,128)(2,1)} %broadcast_in_dim.6), calls=%async_computation | async-start | bytes 4718592 | tf_op jit(solution)/shard_map/all_to_all | solution.py:20
  47.6 26.3 %all-gather = bf16[2304,128]{1,0:T(8,128)(2,1)S(1)} all-gather(bf16[144,128]{1,0:T(8,128)(2,1)S(1)} %get-tuple-element.13), channel_id=2, replica_groups=mesh['x'=4,'zl'=8,'core'=2,'zh'=2,'y'=4] {'zh','zl'}, dimensions={0}, use_global_device_ids=true | all-gather | bytes 626688 | tf_op jit(solution)/shard_map/all_gather | solution.py:149
  73.9 25.8 %all-gather.1 = bf16[2304,128]{1,0:T(8,128)(2,1)} all-gather(bf16[144,128]{1,0:T(8,128)(2,1)S(1)} %collective-permute-done.3), channel_id=3, replica_groups=mesh['x'=4,'zl'=8,'core'=2,'zh'=2,'y'=4] {'zh','zl'}, dimensions={0}, use_global_device_ids=true | all-gather | bytes 626688 | tf_op jit(solution)/shard_map/all_gather | solution.py:150
  99.7 1.1 copy-done.1
  100.8 6.4 %shard_map.101 = bf16[16,160,256]{2,1,0:T(8,128)(2,1)S(1)} custom-call(s32[5]{0:T(128)S(1)} %stack.32.place, f32[2]{0:T(128)S(1)} %pad_maximum_fusion.5.factors, bf16[16,576,128]{2,1,0:T(8,128)(2,1)S(1)} %all-to-all-done.plane, bf16[16,144,128]{2,1,0:T(8,128)(2,1)S(1)} %bitcast.43, bf16[16,144,128]{2,1,0:T(8,128)(2,1)S(1)} %bitcast.44), custom_call_target="tpu_custom_call" | custom-call | tf_op jit(solution)/shard_map/pallas_call | solution.py:106
  107.2 19.0 %all_to_all.25 = bf16[16,160,256]{2,1,0:T(8,128)(2,1)S(1)} all-to-all(bf16[16,160,256]{2,1,0:T(8,128)(2,1)S(1)} %shard_map.101), channel_id=1, replica_groups=mesh['x'=4,'zl'=8,'core'=2,'zh'=2,'y'=4] {'x','y'}, dimensions={0} | all-to-all | bytes 2621440 | tf_op jit(solution)/shard_map/all_to_all | solution.py:153
  126.8 0.8 pad.4
  127.6 3.5 %all-to-all-start.2 = ((bf16[4,56,8,128]{3,2,1,0:T(8,128)(2,1)}), bf16[4,56,8,128]{3,2,1,0:T(8,128)(2,1)S(1)}, u32[]{:S(2)}, u32[]{:S(2)}) async-start(bf16[4,56,8,128]{3,2,1,0:T(8,128)(2,1)} %bitcast.12), calls=%async_computation.2 | async-start | bytes 917504 | tf_op jit(solution)/shard_map/all_to_all | solution.py:164
  131.1 18.1 %collective-permute-start.5 = (f32[8,128]{1,0:T(8,128)S(1)}, f32[8,128]{1,0:T(8,128)S(1)}, u32[]{:S(2)}, u32[]{:S(2)}) collective-permute-start(f32[8,128]{1,0:T(8,128)S(1)} %slice.63), channel_id=1, source_target_pairs={{0,8},{8,0},{1,9},{9,1},{2,10},{10,2},{3,11},{11,3},{4,12},{12,4},... | collective-permute-start | bytes 12296 | tf_op jit(solution)/shard_map/ppermute | solution.py:15
  149.1 0.8 collective-permute-done.5
  150.1 17.4 %all_to_all.26 = f32[8,8,8,128]{3,2,1,0:T(8,128)S(1)} all-to-all(f32[8,8,8,128]{3,2,1,0:T(8,128)S(1)} %pad_maximum_fusion.1), channel_id=1, replica_groups=mesh['x'=4,'zl'=8,'core'=2,'zh'=2,'y'=4] {'zl'}, dimensions={0} | all-to-all | bytes 524288 | tf_op jit(solution)/shard_map/all_to_all | solution.py:167
  167.5 14.6 %all_to_all.27 = bf16[8,7,8,128]{3,2,1,0:T(8,128)(2,1)S(1)} all-to-all(bf16[8,7,8,128]{3,2,1,0:T(8,128)(2,1)S(1)} %broadcast_in_dim.8), channel_id=1, replica_groups=mesh['x'=4,'zl'=8,'core'=2,'zh'=2,'y'=4] {'zl'}, dimensions={0} | all-to-all | bytes 229376 | tf_op jit(solution)/shard_map/all_to_all | solution.py:20
  182.1 15.1 %all-gather.2 = bf16[32,7,8,128]{3,2,1,0:T(8,128)(2,1)S(1)} all-gather(bf16[8,7,8,128]{3,2,1,0:T(8,128)(2,1)S(1)} %all_to_all.27), channel_id=4, replica_groups=mesh['x'=4,'zl'=8,'core'=2,'zh'=2,'y'=4] {'x'}, dimensions={0}, use_global_device_ids=true | all-gather | bytes 573440 | tf_op jit(solution)/shard_map/all_gather | solution.py:171
  197.2 7.5 %collective-permute-start.6 = (bf16[4,8,7,8,128]{4,3,2,1,0:T(8,128)(2,1)S(1)}, bf16[4,8,7,8,128]{4,3,2,1,0:T(8,128)(2,1)S(1)}, u32[]{:S(2)}, u32[]{:S(2)}) collective-permute-start(bf16[4,8,7,8,128]{4,3,2,1,0:T(8,128)(2,1)S(1)} %bitcast.45), channel_id=1, source_target_pairs={{0,8},{8,0},{1,9},{9,1},{2,10},{10,2},{3,11},{11,3},{4,12},{12,4},... | collective-permute-start | bytes 1376264 | tf_op jit(solution)/shard_map/ppermute | solution.py:15
  206.3 1.3 convert_bitcast_fusion
  (44 shorter events, 2.6 us)
Async XLA Ops:
  0.6 1.5 copy-start
  0.6 19.8 %copy-start.2 = (bf16[128,1408]{1,0:T(8,128)(2,1)S(1)}, bf16[128,1408]{1,0:T(8,128)(2,1)}, u32[]{:S(2)}) copy-start(bf16[128,1408]{1,0:T(8,128)(2,1)} %param.7) | copy-start | bytes 1081348
  0.7 19.8 %copy-start.3 = (bf16[128,1408]{1,0:T(8,128)(2,1)S(1)}, bf16[128,1408]{1,0:T(8,128)(2,1)}, u32[]{:S(2)}) copy-start(bf16[128,1408]{1,0:T(8,128)(2,1)} %param.6) | copy-start | bytes 1081348
  3.5 19.9 %collective-permute-start = (bf16[288,128]{1,0:T(8,128)(2,1)S(1)}, bf16[288,128]{1,0:T(8,128)(2,1)S(1)}, u32[]{:S(2)}, u32[]{:S(2)}) collective-permute-start(bf16[288,128]{1,0:T(8,128)(2,1)S(1)} %pad_maximum_fusion.3), channel_id=1, source_target_pairs={{0,4},{4,0},{1,5},{5,1},{2,6},{6,2},{3,7},{7,3},{8,12},{12,8},{9,1... | collective-permute-start | bytes 221192 | tf_op jit(solution)/shard_map/ppermute | solution.py:15
  19.7 7.6 %collective-permute-start.2 = (bf16[288,128]{1,0:T(8,128)(2,1)S(1)}, bf16[288,128]{1,0:T(8,128)(2,1)S(1)}, u32[]{:S(2)}, u32[]{:S(2)}) collective-permute-start(bf16[288,128]{1,0:T(8,128)(2,1)S(1)} %pad_maximum_fusion.3), channel_id=1, source_target_pairs={{0,0},{1,16},{2,32},{3,48},{16,64},{17,80},{18,96},{19,112},{32,1}... | collective-permute-start | bytes 221192 | tf_op jit(solution)/shard_map/ppermute | solution.py:140
  20.5 8.8 %collective-permute-start.4 = (bf16[128,1408]{1,0:T(8,128)(2,1)S(1)}, bf16[128,1408]{1,0:T(8,128)(2,1)S(1)}, u32[]{:S(2)}, u32[]{:S(2)}) collective-permute-start(bf16[128,1408]{1,0:T(8,128)(2,1)S(1)} %broadcast_select_fusion.4), channel_id=1, source_target_pairs={{0,8},{8,0},{1,9},{9,1},{2,10},{10,2},{3,11},{11,3},{4,12},{12,4},... | collective-permute-start | bytes 1081352 | tf_op jit(solution)/shard_map/ppermute | solution.py:15
  23.4 5.9 %collective-permute-start.1 = (bf16[288,128]{1,0:T(8,128)(2,1)S(1)}, bf16[288,128]{1,0:T(8,128)(2,1)S(1)}, u32[]{:S(2)}, u32[]{:S(2)}) collective-permute-start(bf16[288,128]{1,0:T(8,128)(2,1)S(1)} %pad_maximum_fusion.4), channel_id=1, source_target_pairs={{0,8},{8,0},{1,9},{9,1},{2,10},{10,2},{3,11},{11,3},{4,12},{12,4},... | collective-permute-start | bytes 221192 | tf_op jit(solution)/shard_map/ppermute | solution.py:15
  27.4 3.1 %collective-permute-start.3 = (bf16[144,128]{1,0:T(8,128)(2,1)S(1)}, bf16[144,128]{1,0:T(8,128)(2,1)S(1)}, u32[]{:S(2)}, u32[]{:S(2)}) collective-permute-start(bf16[144,128]{1,0:T(8,128)(2,1)S(1)} %get-tuple-element.23), channel_id=1, source_target_pairs={{0,8},{8,0},{1,9},{9,1},{2,10},{10,2},{3,11},{11,3},{4,12},{12,4},... | collective-permute-start | bytes 110600 | tf_op jit(solution)/shard_map/ppermute | solution.py:15
  32.3 67.4 %all-to-all-start = ((bf16[16,576,128]{2,1,0:T(8,128)(2,1)}), bf16[16,576,128]{2,1,0:T(8,128)(2,1)S(1)}, u32[]{:S(2)}, u32[]{:S(2)}) async-start(bf16[16,576,128]{2,1,0:T(8,128)(2,1)} %broadcast_in_dim.6), calls=%async_computation | async-start | bytes 4718592 | tf_op jit(solution)/shard_map/all_to_all | solution.py:20
  99.7 1.1 copy-start.1
  107.2 19.2 %copy-start.4 = (bf16[256,1408]{1,0:T(8,128)(2,1)S(1)}, bf16[256,1408]{1,0:T(8,128)(2,1)}, u32[]{:S(2)}) copy-start(bf16[256,1408]{1,0:T(8,128)(2,1)} %pad_maximum_fusion) | copy-start | bytes 2162692
  127.6 22.4 %all-to-all-start.2 = ((bf16[4,56,8,128]{3,2,1,0:T(8,128)(2,1)}), bf16[4,56,8,128]{3,2,1,0:T(8,128)(2,1)S(1)}, u32[]{:S(2)}, u32[]{:S(2)}) async-start(bf16[4,56,8,128]{3,2,1,0:T(8,128)(2,1)} %bitcast.12), calls=%async_computation.2 | async-start | bytes 917504 | tf_op jit(solution)/shard_map/all_to_all | solution.py:164
  131.1 18.9 %collective-permute-start.5 = (f32[8,128]{1,0:T(8,128)S(1)}, f32[8,128]{1,0:T(8,128)S(1)}, u32[]{:S(2)}, u32[]{:S(2)}) collective-permute-start(f32[8,128]{1,0:T(8,128)S(1)} %slice.63), channel_id=1, source_target_pairs={{0,8},{8,0},{1,9},{9,1},{2,10},{10,2},{3,11},{11,3},{4,12},{12,4},... | collective-permute-start | bytes 12296 | tf_op jit(solution)/shard_map/ppermute | solution.py:15
  197.2 9.0 %collective-permute-start.6 = (bf16[4,8,7,8,128]{4,3,2,1,0:T(8,128)(2,1)S(1)}, bf16[4,8,7,8,128]{4,3,2,1,0:T(8,128)(2,1)S(1)}, u32[]{:S(2)}, u32[]{:S(2)}) collective-permute-start(bf16[4,8,7,8,128]{4,3,2,1,0:T(8,128)(2,1)S(1)} %bitcast.45), channel_id=1, source_target_pairs={{0,8},{8,0},{1,9},{9,1},{2,10},{10,2},{3,11},{11,3},{4,12},{12,4},... | collective-permute-start | bytes 1376264 | tf_op jit(solution)/shard_map/ppermute | solution.py:15
